TPU v7x, 1024 devices: a whole 8x8x8 slice. The times are simulated.
1024 devices in a mesh: rows: 128 (over z, x, core), tm: 8 (over y).
Axes of the slice: x: 8, y: 8, z: 8, core: 2. Of those that a mesh axis runs over, the one named last changes fastest.
Arguments:
- fields: float32 [5, 64, 1024, 4, 128], P(None, 'tm', 'rows'), may hold values from -23 to 23
- channel_mix: float32 [32, 35], replicated, may hold values from -1.5 to 2.5
Outputs:
- running_factor: float32 [8, 256, 256], P('tm')
- coefficients: bfloat16 [64, 32, 1024, 4, 128], P('tm', None, 'rows')
All inputs are finite; a program needn't handle non-finite values.
Results may differ from a plain program's by a relative error of at most 0.0039.
The roundings to bfloat16 on the way count: a program that leaves them out, or rounds other values in their place, can miss the bound.
Values sent between devices are 32-bit elements; how exact they have to be, the bound alone decides.
A program may use at most 128 MiB of HBM per device.

v0:
```python
import jax
import jax.numpy as jnp
from jax import lax
from jax.sharding import PartitionSpec as P


def padded_2(cells, sides, width):
    for axis, dim in sides:
        count = lax.axis_size(axis)
        ends = count - 1
        head = lax.slice_in_dim(cells, 0, width, axis=dim)
        tail = lax.slice_in_dim(cells, cells.shape[dim] - width, cells.shape[dim], axis=dim)
        cells = jnp.concatenate(
            [
                lax.ppermute(tail, axis, [(i, (i + 1) % count) for i in range(ends)]),
                cells,
                lax.ppermute(head, axis, [((i + 1) % count, i) for i in range(ends)]),
            ],
            axis=dim,
        )
    return cells


def prefix(x, axis, combine, identity):
    count, here = (lax.axis_size(axis), lax.axis_index(axis))
    everything = lax.all_gather(x, axis)
    start = jnp.broadcast_to(jnp.asarray(identity, x.dtype), x.shape)

    def turn(k, before):
        reached = k < here
        new = combine(before, everything[k])
        return jnp.where(reached, new, before)

    return lax.fori_loop(0, count, turn, start)


def derivatives(padded):
    center = padded[:, :, 1:-1, 1:-1, 1:-1]
    x_plus = padded[:, :, 2:, 1:-1, 1:-1]
    x_minus = padded[:, :, :-2, 1:-1, 1:-1]
    y_plus = padded[:, :, 1:-1, 2:, 1:-1]
    y_minus = padded[:, :, 1:-1, :-2, 1:-1]
    z_plus = padded[:, :, 1:-1, 1:-1, 2:]
    z_minus = padded[:, :, 1:-1, 1:-1, :-2]
    stacked = jnp.stack(
        [
            center,
            0.5 * (x_plus - x_minus),
            0.5 * (y_plus - y_minus),
            0.5 * (z_plus - z_minus),
            0.25 * (x_plus - 2.0 * center + x_minus),
            0.25 * (y_plus - 2.0 * center + y_minus),
            0.25 * (z_plus - 2.0 * center + z_minus),
        ],
        axis=1,
    )
    shape = stacked.shape
    return stacked.reshape((shape[0] * shape[1],) + shape[2:])


def add_grams(earlier, later):
    return earlier + later


def body(fields, channel_mix):
    grown = padded_2(fields, (("rows", 2),), 1)
    padded = jnp.pad(grown, ((0, 0), (0, 0), (0, 0), (1, 1), (1, 1)))
    stencil = derivatives(padded)
    channels = jnp.einsum(
        "ck,ksxyz->scxyz", channel_mix, stencil, precision=lax.Precision.HIGHEST
    ).astype(jnp.bfloat16)
    width = channels.shape[0] * channels.shape[1]
    local_cells = channels.shape[2] * channels.shape[3] * channels.shape[4]
    features = channels.reshape(width, local_cells)
    gram = lax.dot_general(
        features, features, (((1,), (1,)), ((), ())), preferred_element_type=jnp.float32
    )
    group_gram = lax.psum(gram, "rows")
    before = prefix(group_gram, "tm", add_grams, jnp.zeros_like(group_gram))
    running_gram = before + group_gram
    row_count = (lax.axis_index("tm") + 1).astype(jnp.float32) * jnp.float32(
        local_cells * lax.axis_size("rows")
    )
    factor = jnp.linalg.cholesky(running_gram / row_count)
    solved = lax.linalg.triangular_solve(
        factor, features.astype(jnp.float32), left_side=True, lower=True
    )
    coefficients = solved.reshape(channels.shape).astype(jnp.bfloat16)
    return (factor[None], coefficients)


def solution(mesh):
    return jax.shard_map(
        body,
        mesh=mesh,
        in_specs=(P(None, "tm", "rows", None, None), P()),
        out_specs=(P("tm", None, None), P("tm", None, "rows", None, None)),
        check_vma=False,
    )
```

profile of v0, /device:TPU:113, one launch (start us, length us, event | category | flops | bytes accessed | tf_op | source)
XLA Modules:
  0.0 389.8 jit_solution(9860616846731186712)
XLA Ops:
  7.2 0.9 fusion.18
  8.2 2.6 collective-permute-start
  10.8 3.0 collective-permute-start.1
  13.8 1.1 bitcast_dynamic-update-slice_fusion.7
  14.9 1.1 copy.9
  16.1 1.8 select_maximum_fusion
  19.9 6.7 %convert_bitcast_fusion = bf16[8,32,8,4,128]{4,1,3,2,0:T(8,128)(2,1)S(1)} fusion(f32[35,8,8,4,128]{4,2,3,1,0:T(8,128)S(1)} %bitcast.77, f32[32,35]{1,0:T(8,128)S(1)} %copy-done), kind=kOutput, calls=%fused_computation.17 | convolution fusion | flops 441450496 | bytes 6689152 | tf_op jit(solution)/shard_map/ck,ksxyz->scxyz/dot_general | solution.py:69
  26.6 2.4 copy.22
  29.0 4.5 %reshape.32 = bf16[256,4096]{1,0:T(8,128)(2,1)} reshape(bf16[8,32,8,4,128]{4,3,2,1,0:T(4,128)(2,1)} %copy.22) | data formatting | bytes 4194304 | tf_op jit(solution)/shard_map/reshape | solution.py:74
  33.4 3.7 fusion.20
  37.4 213.4 %all-reduce.4.cloned.1.call-done = f32[256,256]{0,1:T(8,128)} async-done(((f32[256,256]{0,1:T(8,128)}), f32[256,256]{0,1:T(8,128)}) %all-reduce.4.cloned.1.call-update) | async-done | bytes 262160 | tf_op jit(solution)/shard_map/psum | solution.py:78
  251.4 1.8 fusion.17
  253.7 1.6 triangular_solve.53
  255.3 2.7 copy.28
  258.0 2.1 reshape.52
  260.1 32.5 %all-gather.3.cloned.1.call-done = f32[2048,256]{0,1:T(8,128)} async-done(((f32[256,256]{0,1:T(8,128)}), f32[2048,256]{0,1:T(8,128)}) %all-gather.3.cloned.1.call-update) | async-done | bytes 2097168 | tf_op jit(solution)/shard_map/all_gather | solution.py:26
  292.6 2.9 copy.31
  295.5 8.5 %while.16 = (s32[]{:T(128)}, f32[256,256]{1,0:T(8,128)S(1)}, s32[]{:T(128)}, f32[8,256,256]{2,1,0:T(8,128)}, s32[]{:T(128)}, /*index=5*/s32[]{:T(128)}) while((s32[]{:T(128)}, f32[256,256]{1,0:T(8,128)S(1)}, s32[]{:T(128)}, f32[8,256,256]{2,1,0:T(8,128)}, s32[]{:T(128)}, /*index=5*/s32[]{:T(128)}) %tuple.70), condition=%wide.region_2.3_spmd.clone, body=%wide.region_1.2_spmd.clone.sunk | while | flops 196612 | bytes 786525 | solution.py:34
  295.5 1.1 add_select_fusion.2
  296.7 1.0 add_select_fusion.2
  297.7 1.0 add_select_fusion.2
  298.8 1.0 add_select_fusion.2
  299.8 1.0 add_select_fusion.2
  300.9 1.0 add_select_fusion.2
  302.0 1.0 add_select_fusion.2
  303.0 1.0 add_select_fusion.2
  304.1 0.8 copy.25
  304.9 1.1 add_divide_fusion
  306.0 0.8 copy.26
  306.8 1.0 fusion.7
  307.8 0.7 copy-done.5
  308.5 11.7 %cholesky.49 = f32[128,128]{1,0:T(8,128)S(1)} custom-call(f32[128,128]{1,0:T(8,128)S(1)} %cholesky.115), custom_call_target="Cholesky" | custom-call | tf_op jit(solution)/shard_map/jit(cholesky)/cholesky | solution.py:84
  320.8 9.8 %custom-call.14 = f32[1,128,128]{1,2,0:T(8,128)S(1)} custom-call(f32[1,128,128]{2,1,0:T(8,128)S(1)} %get-tuple-element.140), custom_call_target="InvertDiagBlocksLowerTriangular" | custom-call | tf_op jit(solution)/shard_map/jit(cholesky)/cholesky | solution.py:84
  330.6 1.0 constant_dynamic-update-slice_fusion.1
  331.7 1.1 convolution_subtract_fusion.1
  332.8 11.7 %cholesky.103 = f32[128,128]{1,0:T(8,128)S(1)} custom-call(f32[128,128]{1,0:T(8,128)S(1)} %convolution_subtract_fusion.1), custom_call_target="Cholesky" | custom-call | tf_op jit(solution)/shard_map/jit(cholesky)/cholesky | solution.py:84
  344.5 1.4 compare_reduce_fusion
  347.1 1.7 fusion.8
  348.8 0.7 triangular_solve.48
  349.5 5.0 %while.15 = (s32[]{:T(128)}, f32[256,256]{1,0:T(8,128)S(1)}, s32[2,2]{1,0:T(2,128)S(1)}, f32[2,128,128]{2,1,0:T(8,128)}, s32[]{:T(128)}) while((s32[]{:T(128)}, f32[256,256]{1,0:T(8,128)S(1)}, s32[2,2]{1,0:T(2,128)S(1)}, f32[2,128,128]{2,1,0:T(8,128)}, s32[]{:T(128)}) %tuple.63), condition=%wide.while_cond, body=%wide.while_body.sunk | while | flops 2 | bytes 132705 | solution.py:85
  349.5 0.6 fusion.29
  350.1 1.9 bitcast_dynamic-update-slice_fusion.9
  352.6 1.9 bitcast_dynamic-update-slice_fusion.9
  354.6 20.5 %custom-call.15 = f32[2,128,128]{1,2,0:T(8,128)S(1)} custom-call(f32[2,128,128]{2,1,0:T(8,128)} %get-tuple-element.89), custom_call_target="InvertDiagBlocksLowerTriangular" | custom-call | tf_op jit(solution)/shard_map/triangular_solve | solution.py:85
  375.1 1.0 fusion.19
  376.1 2.0 convolution_subtract_fusion
  378.1 1.9 convolution_convert_fusion
  380.2 2.7 convert_element_type.19
  (35 shorter events, 4.8 us)
Async XLA Ops:
  7.2 12.7 %copy-start = (f32[32,35]{1,0:T(8,128)S(1)}, f32[32,35]{1,0:T(8,128)}, u32[]{:S(2)}) copy-start(f32[32,35]{1,0:T(8,128)} %param.5) | copy-start | bytes 13444
  7.2 243.6 %all-reduce.4.cloned.1.call-start = ((), (), s32[]{:S(2)}) async-start(), calls=%async_computation | async-start | bytes 524288 | tf_op jit(solution)/shard_map/psum | solution.py:78
  8.2 7.9 %collective-permute-start = (f32[5,8,1,4,128]{4,2,3,1,0:T(1,128)S(1)}, f32[5,8,1,4,128]{4,2,3,1,0:T(1,128)S(1)}, u32[]{:S(2)}, u32[]{:S(2)}) collective-permute-start(f32[5,8,1,4,128]{4,2,3,1,0:T(1,128)S(1)} %bitcast.80), channel_id=1, source_target_pairs={{8,0},{16,8},{24,16},{32,24},{40,32},{48,40},{56,48},{64,56},{72,6... | collective-permute-start | bytes 245768 | tf_op jit(solution)/shard_map/ppermute | solution.py:17
  10.8 5.3 %collective-permute-start.1 = (f32[5,8,1,4,128]{4,2,3,1,0:T(1,128)S(1)}, f32[5,8,1,4,128]{4,2,3,1,0:T(1,128)S(1)}, u32[]{:S(2)}, u32[]{:S(2)}) collective-permute-start(f32[5,8,1,4,128]{4,2,3,1,0:T(1,128)S(1)} %bitcast.79), channel_id=1, source_target_pairs={{0,8},{8,16},{16,24},{24,32},{32,40},{40,48},{48,56},{56,64},{64,7... | collective-permute-start | bytes 245768 | tf_op jit(solution)/shard_map/ppermute | solution.py:15
  17.9 1.3 copy-start.1
  37.1 255.5 %all-gather.3.cloned.1.call-start = ((), (), s32[]{:S(2)}) async-start(), calls=%async_computation.1 | async-start | bytes 2359296 | tf_op jit(solution)/shard_map/all_gather | solution.py:26
  253.2 2.2 copy-start.2
  295.5 79.5 %copy-start.3 = (bf16[128,4096]{1,0:T(8,128)(2,1)S(1)}, bf16[128,4096]{1,0:T(8,128)(2,1)}, u32[]{:S(2)}) copy-start(bf16[128,4096]{1,0:T(8,128)(2,1)} %triangular_solve.53) | copy-start | bytes 3145732
  307.8 0.7 copy-start.5
  344.5 2.6 copy-start.4
Sparse Core Ops, SparseCore 0:
  37.2 213.4 all-reduce.3
  253.4 39.1 all-gather.2
where the time goes:
time: 397 us; the launch traced here: 390 us
  waiting for transfers between devices  246 us (62%)
  other arithmetic  74 us (19%)
  local copies, waits for them, and re-layouts  30.8 us (8%)
  matrix products  17.4 us (4%)
  between operations  15.5 us (4%)
  starting transfers between devices  5.86 us (1%)
    psum x1, waiting for transfers between devices, body(): group_gram = lax.psum(gram, 'rows')  213 us
    another operation x6, other arithmetic, body(): factor = jnp.linalg.cholesky(running_gram / row_count)  35.2 us
    all_gather x1, waiting for transfers between devices, prefix(): everything = lax.all_gather(x, axis)  32.5 us
    another operation x5, other arithmetic, body(): lax.linalg.triangular_solve(factor, features.astype(jnp.float32), left_si...  24.7 us
    select_n x8, other arithmetic, turn(): return jnp.where(reached, new, before)  8.36 us
  transfers between devices with their start and end apart: 4, of which 2 were waited for; matrix products, arithmetic and copies ran while one was open for 3% of the time, Pallas kernels for 0%

commit v1 on v0

--- a/solution.py
+++ b/solution.py
@@ -1,7 +1,14 @@
+import functools
+import math
+
 import jax
 import jax.numpy as jnp
 from jax import lax
+from jax.experimental import pallas as pl
+from jax.experimental.pallas import tpu as pltpu
 from jax.sharding import PartitionSpec as P
+
+MESH = pl.DeviceIdType.MESH
 
 
 def padded_2(cells, sides, width):
@@ -19,19 +26,6 @@
             axis=dim,
         )
     return cells
-
-
-def prefix(x, axis, combine, identity):
-    count, here = (lax.axis_size(axis), lax.axis_index(axis))
-    everything = lax.all_gather(x, axis)
-    start = jnp.broadcast_to(jnp.asarray(identity, x.dtype), x.shape)
-
-    def turn(k, before):
-        reached = k < here
-        new = combine(before, everything[k])
-        return jnp.where(reached, new, before)
-
-    return lax.fori_loop(0, count, turn, start)
 
 
 def derivatives(padded):
@@ -58,8 +52,180 @@
     return stacked.reshape((shape[0] * shape[1],) + shape[2:])
 
 
-def add_grams(earlier, later):
-    return earlier + later
+def running_kernel(
+    side, steps, gram_ref, out_ref,
+    stack, pair_in, mine, got_a, got_b, got_y, whole,
+    pair_send, pair_recv, a_send, a_recv, b_send, b_recv,
+    y_send, y_recv, g_send, g_recv, f_send, f_recv,
+):
+    here = lax.axis_index("rows")
+    t = lax.axis_index("tm")
+    core = here % 2
+    chip = here // 2
+    z, x = chip // side, chip % side
+    a = (1 - core) * x + core * z
+    b = (1 - core) * z + core * x
+    a_step = (1 - core) + core * side
+    b_step = (1 - core) * side + core
+    half = stack.shape[1]
+    piece = half // side
+
+    def at_a(k):
+        return {"rows": 2 * (k * a_step + b * b_step) + core}
+
+    def at_b(k):
+        return {"rows": 2 * (a * a_step + k * b_step) + core}
+
+    def at_t(k):
+        return {"tm": k}
+
+    partner = {"rows": 2 * chip + 1 - core}
+
+    def copy(src, dst, send, recv, to):
+        return pltpu.make_async_remote_copy(
+            src_ref=src, dst_ref=dst, send_sem=send, recv_sem=recv,
+            device_id=to, device_id_type=MESH,
+        )
+
+    barrier = pltpu.get_barrier_semaphore()
+    pl.semaphore_signal(barrier, inc=1, device_id=partner, device_id_type=MESH)
+    for d in range(1, side):
+        pl.semaphore_signal(barrier, inc=1, device_id=at_a((a + d) % side), device_id_type=MESH)
+        pl.semaphore_signal(barrier, inc=1, device_id=at_b((b + d) % side), device_id_type=MESH)
+    for d in range(1, steps):
+        pl.semaphore_signal(barrier, inc=1, device_id=at_t((t + d) % steps), device_id_type=MESH)
+
+    edge = gram_ref.shape[0] // 2
+    flat = [gram_ref[:edge, :edge], gram_ref[edge:, :edge], gram_ref[edge:, edge:]]
+    cut = edge // 2
+    stack[0, :edge] = flat[0]
+    stack[0, edge:] = flat[1][:cut]
+    stack[1, :cut] = flat[1][cut:]
+    stack[1, cut:] = flat[2]
+
+    pl.semaphore_wait(barrier, 2 * (side - 1) + steps)
+
+    sends = []
+    pair = copy(stack.at[1 - core], pair_in, pair_send, pair_recv, partner)
+    pair.start()
+    sends.append(pair)
+    pair.wait_recv()
+    mine[...] = (stack[core] + pair_in[...]).reshape(mine.shape)
+
+    for d in range(1, side):
+        k = (a + d) % side
+        c = copy(mine.at[k], got_a.at[a], a_send.at[d], a_recv.at[a], at_a(k))
+        c.start()
+        sends.append(c)
+    total = mine[a]
+    for d in range(1, side):
+        k = (a + d) % side
+        copy(mine.at[a], got_a.at[k], a_send.at[d], a_recv.at[k], at_a(k)).wait_recv()
+        total = total + got_a[k]
+    got_b[b] = total
+
+    for d in range(1, side):
+        k = (b + d) % side
+        c = copy(got_b.at[b], got_b.at[b], b_send.at[d], b_recv.at[b], at_b(k))
+        c.start()
+        sends.append(c)
+    for d in range(1, side):
+        k = (b + d) % side
+        copy(got_b.at[b], got_b.at[k], b_send.at[d], b_recv.at[k], at_b(k)).wait_recv()
+    total = got_b[0]
+    for k in range(1, side):
+        total = total + got_b[k]
+    got_y[t] = total
+
+    for d in range(1, steps):
+        k = t + d
+
+        @pl.when(k < steps)
+        def _():
+            copy(got_y.at[t], got_y.at[t], y_send.at[d], y_recv.at[t], at_t(k)).start()
+
+    whole[core, a] = jnp.zeros_like(total)
+    for k in range(steps):
+
+        @pl.when(k < t)
+        def _():
+            copy(got_y.at[k], got_y.at[k], y_send.at[0], y_recv.at[k], at_t(k)).wait_recv()
+
+        @pl.when(k <= t)
+        def _():
+            whole[core, a] += got_y[k]
+
+    def forward(k):
+        return copy(whole.at[core, k], whole.at[core, k], f_send.at[k], f_recv.at[k], partner)
+
+    for d in range(1, side):
+        k = (a + d) % side
+        c = copy(whole.at[core, a], whole.at[core, a], g_send.at[d], g_recv.at[a], at_a(k))
+        c.start()
+        sends.append(c)
+    c = forward(a)
+    c.start()
+    sends.append(c)
+    for d in range(1, side):
+        k = (a + d) % side
+        copy(whole.at[core, a], whole.at[core, k], g_send.at[d], g_recv.at[k], at_a(k)).wait_recv()
+        c = forward(k)
+        c.start()
+        sends.append(c)
+    for k in range(side):
+        copy(
+            whole.at[core, k], whole.at[1 - core, k], f_send.at[k], f_recv.at[k], partner
+        ).wait_recv()
+
+    first = whole[0].reshape(half, edge)
+    second = whole[1].reshape(half, edge)
+    out_ref[:edge, :edge] = first[:edge]
+    out_ref[edge:edge + cut, :edge] = first[edge:]
+    out_ref[edge + cut:, :edge] = second[:cut]
+    out_ref[edge:, edge:] = second[cut:]
+    out_ref[:edge, edge:] = jnp.concatenate([first[edge:], second[:cut]], axis=0).T
+
+    for c in sends:
+        c.wait_send()
+    for d in range(1, steps):
+        k = t + d
+
+        @pl.when(k < steps)
+        def _():
+            copy(got_y.at[t], got_y.at[t], y_send.at[d], y_recv.at[t], at_t(k)).wait_send()
+
+
+def running_sum(gram):
+    side = math.isqrt(lax.axis_size("rows") // 2)
+    steps = lax.axis_size("tm")
+    width = gram.shape[0]
+    edge = width // 2
+    half = 3 * edge // 2
+    piece = half // side
+    dma = pltpu.SemaphoreType.DMA
+    f32 = jnp.float32
+    return pl.pallas_call(
+        functools.partial(running_kernel, side, steps),
+        out_shape=jax.ShapeDtypeStruct((width, width), f32),
+        in_specs=[pl.BlockSpec(memory_space=pltpu.VMEM)],
+        out_specs=pl.BlockSpec(memory_space=pltpu.VMEM),
+        scratch_shapes=[
+            pltpu.VMEM((2, half, edge), f32),
+            pltpu.VMEM((half, edge), f32),
+            pltpu.VMEM((side, piece, edge), f32),
+            pltpu.VMEM((side, piece, edge), f32),
+            pltpu.VMEM((side, piece, edge), f32),
+            pltpu.VMEM((steps, piece, edge), f32),
+            pltpu.VMEM((2, side, piece, edge), f32),
+            dma, dma,
+            dma((side,)), dma((side,)),
+            dma((side,)), dma((side,)),
+            dma((steps,)), dma((steps,)),
+            dma((side,)), dma((side,)),
+            dma((side,)), dma((side,)),
+        ],
+        compiler_params=pltpu.CompilerParams(collective_id=0, has_side_effects=True),
+    )(gram)
 
 
 def body(fields, channel_mix):
@@ -75,13 +241,11 @@
     gram = lax.dot_general(
         features, features, (((1,), (1,)), ((), ())), preferred_element_type=jnp.float32
     )
-    group_gram = lax.psum(gram, "rows")
-    before = prefix(group_gram, "tm", add_grams, jnp.zeros_like(group_gram))
-    running_gram = before + group_gram
+    running_gram = running_sum(gram)
     row_count = (lax.axis_index("tm") + 1).astype(jnp.float32) * jnp.float32(
         local_cells * lax.axis_size("rows")
     )
-    factor = jnp.linalg.cholesky(running_gram / row_count)
+    factor = lax.linalg.cholesky(running_gram / row_count, symmetrize_input=False)
     solved = lax.linalg.triangular_solve(
         factor, features.astype(jnp.float32), left_side=True, lower=True
     )

time: 397 us -> 160 us (0.40); the launches traced: 390 us -> 159 us
  waiting for transfers between devices: 246 us -> 0.01 us
  Pallas kernels: 0 us -> 42.6 us
  between operations: 15.5 us -> 2.2 us
  other arithmetic: 74 us -> 64.8 us
    psum x1 -> x0, waiting for transfers between devices: 213 us -> none  [body(): group_gram = lax.psum(gram, 'rows')]
    pallas_call x0 -> x1, Pallas kernels: none -> 42.6 us  [running_sum(): pl.pallas_call(functools.partial(running_kernel, side, steps), out_shape=...]
    all_gather x1 -> x0, waiting for transfers between devices: 32.5 us -> none  [prefix(): everything = lax.all_gather(x, axis)]
    select_n x8 -> x0, other arithmetic: 8.36 us -> none  [turn(): return jnp.where(reached, new, before)]
  transfers between devices with their start and end apart: 4 -> 2, of which waited for: 2 -> 0; matrix products, arithmetic and copies ran while one was open for 3% -> 2% of each run, Pallas kernels for 0% -> 0%
where the time goes in v1:
time: 160 us; the launch traced here: 159 us
  other arithmetic  64.8 us (40%)
  Pallas kernels  42.6 us (27%)
  local copies, waits for them, and re-layouts  28.2 us (18%)
  matrix products  15.2 us (10%)
  starting transfers between devices  5.6 us (4%)
  between operations  2.2 us (1%)
    pallas_call x1, Pallas kernels, running_sum(): pl.pallas_call(functools.partial(running_kernel, side, steps), out_shape=...  42.6 us
    another operation x6, other arithmetic, body(): lax.linalg.cholesky(running_gram / row_count, symmetrize_input=False)  35.2 us
    another operation x5, other arithmetic, body(): lax.linalg.triangular_solve(factor, features.astype(jnp.float32), left_si...  24.8 us
    another operation x5, local copies, waits for them, and re-layouts, body(): lax.linalg.triangular_solve(factor, features.astype(jnp.float32), left_si...  9.74 us
    dot_general x1, matrix products, body(): jnp.einsum('ck,ksxyz->scxyz', channel_mix, stencil, precision=lax.Precisi...  6.68 us
    another operation x6, local copies, waits for them, and re-layouts  5.26 us
    another operation x3, matrix products, body(): lax.linalg.triangular_solve(factor, features.astype(jnp.float32), left_si...  4.94 us
    unnamed x16, local copies, waits for them, and re-layouts  3.88 us
  transfers between devices with their start and end apart: 2, of which 0 were waited for; matrix products, arithmetic and copies ran while one was open for 2% of the time, Pallas kernels for 0%

profile of v1, /device:TPU:113, one launch (start us, length us, event | category | flops | bytes accessed | tf_op | source)
XLA Modules:
  0.0 158.7 jit_solution(1908574654737271125)
XLA Ops:
  0.6 0.0 copy-start
  0.6 0.9 fusion.17
  1.6 2.6 %collective-permute-start = (f32[5,8,1,4,128]{4,2,3,1,0:T(1,128)S(1)}, f32[5,8,1,4,128]{4,2,3,1,0:T(1,128)S(1)}, u32[]{:S(2)}, u32[]{:S(2)}) collective-permute-start(f32[5,8,1,4,128]{4,2,3,1,0:T(1,128)S(1)} %bitcast.70), channel_id=1, source_target_pairs={{8,0},{16,8},{24,16},{32,24},{40,32},{48,40},{56,48},{64,56},{72,6... | collective-permute-start | bytes 245768 | tf_op jit(solution)/shard_map/ppermute | solution.py:24
  4.2 3.0 %collective-permute-start.1 = (f32[5,8,1,4,128]{4,2,3,1,0:T(1,128)S(1)}, f32[5,8,1,4,128]{4,2,3,1,0:T(1,128)S(1)}, u32[]{:S(2)}, u32[]{:S(2)}) collective-permute-start(f32[5,8,1,4,128]{4,2,3,1,0:T(1,128)S(1)} %bitcast.69), channel_id=1, source_target_pairs={{0,8},{8,16},{16,24},{24,32},{32,40},{40,48},{48,56},{56,64},{64,7... | collective-permute-start | bytes 245768 | tf_op jit(solution)/shard_map/ppermute | solution.py:22
  7.2 1.1 copy.5
  8.4 2.0 %bitcast_dynamic-update-slice_fusion.7 = f32[5,7,8,8,4,128]{5,3,4,2,1,0:T(8,128)} fusion(f32[5,8,8,4,128]{4,3,2,1,0:T(4,128)} %param.2), kind=kLoop, calls=%fused_computation.27 | loop fusion | bytes 1310720
  10.4 0.6 iota_multiply_fusion
  11.0 1.8 %select_maximum_fusion = f32[5,8,10,6,130]{4,2,3,1,0:T(8,128)S(1)} fusion(f32[5,8,1,4,128]{4,2,3,1,0:T(1,128)S(1)} %collective-permute-done, f32[5,8,8,4,128]{4,2,3,1,0:T(8,128)S(1)} %copy.5, f32[5,8,1,4,128]{4,2,3,1,0:T(1,128)S(1)} %collective-permute-done.1), kind=kLoop, calls=%fused_computation.10 | loop fusion | flops 4680000 | bytes 2067200 | tf_op jit(solution)/shard_map/concatenate | solution.py:20
  12.8 0.0 copy-start.1
  12.8 0.3 bitcast_dynamic-update-slice_fusion.5
  13.1 0.4 bitcast_dynamic-update-slice_fusion.4
  13.5 0.2 bitcast_dynamic-update-slice_fusion.3
  13.7 0.3 bitcast_dynamic-update-slice_fusion.2
  14.0 0.4 bitcast_dynamic-update-slice_fusion.1
  14.4 0.3 bitcast_dynamic-update-slice_fusion.6
  14.7 6.7 %convert_bitcast_fusion = bf16[8,32,8,4,128]{4,1,3,2,0:T(8,128)(2,1)S(1)} fusion(f32[35,8,8,4,128]{4,2,3,1,0:T(8,128)S(1)} %bitcast.68, f32[32,35]{1,0:T(8,128)S(1)} %copy-done), kind=kOutput, calls=%fused_computation.16 | convolution fusion | flops 441450496 | bytes 6689152 | tf_op jit(solution)/shard_map/ck,ksxyz->scxyz/dot_general | solution.py:235
  21.4 2.4 %copy.18 = bf16[8,32,8,4,128]{4,3,2,1,0:T(4,128)(2,1)} copy(bf16[8,32,8,4,128]{4,1,3,2,0:T(8,128)(2,1)S(1)} %convert_bitcast_fusion) | data formatting | bytes 4194304 | tf_op jit(solution)/shard_map/convert_element_type | solution.py:237
  23.8 1.8 %fusion.16 = (bf16[4,32,8,4,128]{4,1,3,2,0:T(8,128)(2,1)S(1)}, f32[4,32,8,4,128]{4,1,3,2,0:T(8,128)}) fusion(bf16[8,32,8,4,128]{4,1,3,2,0:T(8,128)(2,1)S(1)} %convert_bitcast_fusion), kind=kLoop, calls=%fused_computation.52 | loop fusion | flops 524288 | bytes 5242880 | tf_op jit(solution)/shard_map/triangular_solve | solution.py:249
  25.7 3.3 %reshape.30 = bf16[256,4096]{1,0:T(8,128)(2,1)S(1)} reshape(bf16[8,32,8,4,128]{4,3,2,1,0:T(4,128)(2,1)} %copy.18) | data formatting | bytes 4194304 | tf_op jit(solution)/shard_map/reshape | solution.py:240
  29.0 1.4 fusion.19.gram_ref
  30.4 42.6 %shard_map.41 = f32[256,256]{1,0:T(8,128)} custom-call(f32[256,256]{1,0:T(8,128)} %fusion.19.gram_ref), custom_call_target="tpu_custom_call" | custom-call | tf_op jit(solution)/shard_map/pallas_call | solution.py:207
  73.1 1.1 broadcast_divide_fusion
  74.2 0.0 copy-start.6
  74.2 0.7 copy-done.6
  74.9 11.7 %cholesky.50 = f32[128,128]{1,0:T(8,128)S(1)} custom-call(f32[128,128]{1,0:T(8,128)S(1)} %cholesky.118), custom_call_target="Cholesky" | custom-call | tf_op jit(solution)/shard_map/cholesky | solution.py:248
  86.6 0.6 select_reduce_fusion.1
  87.2 9.8 %custom-call.11 = f32[1,128,128]{1,2,0:T(8,128)S(1)} custom-call(f32[1,128,128]{2,1,0:T(8,128)S(1)} %get-tuple-element.29), custom_call_target="InvertDiagBlocksLowerTriangular" | custom-call | tf_op jit(solution)/shard_map/cholesky | solution.py:248
  97.0 1.0 constant_dynamic-update-slice_fusion.1
  98.0 1.1 convolution_subtract_fusion.1
  99.2 11.7 %cholesky.105 = f32[128,128]{1,0:T(8,128)S(1)} custom-call(f32[128,128]{1,0:T(8,128)S(1)} %convolution_subtract_fusion.1), custom_call_target="Cholesky" | custom-call | tf_op jit(solution)/shard_map/cholesky | solution.py:248
  110.9 1.4 compare_reduce_fusion
  113.6 1.7 %fusion.7 = (f32[256,256]{1,0:T(8,128)S(1)}, f32[1,256,256]{2,1,0:T(8,128)}) fusion(f32[256,256]{1,0:T(8,128)} %copy-done.5, pred[]{:T(512)S(6)} %cholesky.110), kind=kLoop, calls=%fused_computation.30 | loop fusion | flops 262144 | bytes 786433 | tf_op jit(solution)/shard_map/triangular_solve | solution.py:249
  115.3 0.7 triangular_solve.48
  116.0 5.3 %while.1 = (s32[]{:T(128)}, f32[256,256]{1,0:T(8,128)S(1)}, s32[2,2]{1,0:T(2,128)S(1)}, f32[2,128,128]{2,1,0:T(8,128)}, s32[]{:T(128)}) while((s32[]{:T(128)}, f32[256,256]{1,0:T(8,128)S(1)}, s32[2,2]{1,0:T(2,128)S(1)}, f32[2,128,128]{2,1,0:T(8,128)}, s32[]{:T(128)}) %tuple.31), condition=%wide.while_cond, body=%wide.while_body.sunk | while | flops 2 | bytes 132705 | solution.py:249
  116.1 0.6 fusion.28
  116.6 2.0 %bitcast_dynamic-update-slice_fusion.9 = f32[2,128,128]{2,1,0:T(8,128)} fusion(f32[2,128,128]{2,1,0:T(8,128)} %get-tuple-element.73, s32[]{:T(128)} %get-tuple-element.70, f32[256,256]{1,0:T(8,128)S(1)} %get-tuple-element.76, s32[]{:T(128)} %bitcast.66, s32[]{:T(128)} %bitcast.67), kind=kLoop, calls=%fused_computation.clone.1 | loop fusion | bytes 132608 | tf_op jit(solution)/shard_map/triangular_solve
  118.7 0.6 fusion.28
  119.3 2.0 %bitcast_dynamic-update-slice_fusion.9 = f32[2,128,128]{2,1,0:T(8,128)} fusion(f32[2,128,128]{2,1,0:T(8,128)} %get-tuple-element.73, s32[]{:T(128)} %get-tuple-element.70, f32[256,256]{1,0:T(8,128)S(1)} %get-tuple-element.76, s32[]{:T(128)} %bitcast.66, s32[]{:T(128)} %bitcast.67), kind=kLoop, calls=%fused_computation.clone.1 | loop fusion | bytes 132608 | tf_op jit(solution)/shard_map/triangular_solve
  121.3 20.5 %custom-call.12 = f32[2,128,128]{1,2,0:T(8,128)S(1)} custom-call(f32[2,128,128]{2,1,0:T(8,128)} %get-tuple-element.9), custom_call_target="InvertDiagBlocksLowerTriangular" | custom-call | tf_op jit(solution)/shard_map/triangular_solve | solution.py:249
  141.8 1.5 copy.19
  143.3 2.6 %triangular_solve.53 = bf16[128,4096]{1,0:T(8,128)(2,1)} reshape(bf16[4,32,8,4,128]{4,3,2,1,0:T(4,128)(2,1)} %copy.19) | data formatting | bytes 2097152 | tf_op jit(solution)/shard_map/triangular_solve | solution.py:249
  145.9 2.7 %copy.20 = f32[4,32,8,4,128]{4,3,2,1,0:T(4,128)} copy(f32[4,32,8,4,128]{4,1,3,2,0:T(8,128)S(1)} %copy-done.2) | data formatting | bytes 4194304 | tf_op jit(solution)/shard_map/triangular_solve | solution.py:249
  148.6 2.2 %reshape.50 = f32[128,4096]{1,0:T(8,128)S(1)} reshape(f32[4,32,8,4,128]{4,3,2,1,0:T(4,128)} %copy.20) | data formatting | bytes 4194304 | tf_op jit(solution)/shard_map/triangular_solve | solution.py:249
  150.8 1.0 fusion.18
  151.9 2.0 %convolution_subtract_fusion = f32[128,4096]{1,0:T(8,128)S(1)} fusion(f32[128,4096]{1,0:T(8,128)S(1)} %reshape.50, f32[128,4096]{1,0:T(8,128)S(1)} %get-tuple-element.33, f32[256,256]{1,0:T(8,128)S(1)} %get-tuple-element.80), kind=kOutput, calls=%fused_computation.8 | convolution fusion | flops 805830656 | bytes 6356992 | tf_op jit(solution)/shard_map/triangular_solve | solution.py:249
  153.8 1.9 %convolution_convert_fusion = bf16[128,4096]{1,0:T(8,128)(2,1)S(1)} fusion(f32[128,4096]{1,0:T(8,128)S(1)} %convolution_subtract_fusion, f32[2,128,128]{1,2,0:T(8,128)S(1)} %custom-call.12), kind=kOutput, calls=%fused_computation.9 | convolution fusion | flops 805830656 | bytes 3211264 | tf_op jit(solution)/shard_map/triangular_solve | solution.py:249
  155.8 0.2 pad_maximum_fusion
  156.0 2.7 %convert_element_type.19 = bf16[8,32,8,4,128]{4,3,2,1,0:T(4,128)(2,1)} reshape(bf16[256,4096]{1,0:T(8,128)(2,1)S(1)} %pad_maximum_fusion) | data formatting | bytes 4194304 | tf_op jit(solution)/shard_map/convert_element_type | solution.py:252
  (18 shorter events, 0.1 us)
Async XLA Ops:
  0.6 14.1 %copy-start = (f32[32,35]{1,0:T(8,128)S(1)}, f32[32,35]{1,0:T(8,128)}, u32[]{:S(2)}) copy-start(f32[32,35]{1,0:T(8,128)} %param.3) | copy-start | bytes 13444
  1.6 9.4 %collective-permute-start = (f32[5,8,1,4,128]{4,2,3,1,0:T(1,128)S(1)}, f32[5,8,1,4,128]{4,2,3,1,0:T(1,128)S(1)}, u32[]{:S(2)}, u32[]{:S(2)}) collective-permute-start(f32[5,8,1,4,128]{4,2,3,1,0:T(1,128)S(1)} %bitcast.70), channel_id=1, source_target_pairs={{8,0},{16,8},{24,16},{32,24},{40,32},{48,40},{56,48},{64,56},{72,6... | collective-permute-start | bytes 245768 | tf_op jit(solution)/shard_map/ppermute | solution.py:24
  4.2 6.8 %collective-permute-start.1 = (f32[5,8,1,4,128]{4,2,3,1,0:T(1,128)S(1)}, f32[5,8,1,4,128]{4,2,3,1,0:T(1,128)S(1)}, u32[]{:S(2)}, u32[]{:S(2)}) collective-permute-start(f32[5,8,1,4,128]{4,2,3,1,0:T(1,128)S(1)} %bitcast.69), channel_id=1, source_target_pairs={{0,8},{8,16},{16,24},{24,32},{32,40},{40,48},{48,56},{56,64},{64,7... | collective-permute-start | bytes 245768 | tf_op jit(solution)/shard_map/ppermute | solution.py:22
  10.4 2.4 %copy-start.3 = (f32[5,7,8,8,4,128]{5,3,4,2,1,0:T(8,128)S(1)}, f32[5,7,8,8,4,128]{5,3,4,2,1,0:T(8,128)}, u32[]{:S(2)}) copy-start(f32[5,7,8,8,4,128]{5,3,4,2,1,0:T(8,128)} %bitcast_dynamic-update-slice_fusion.7) | copy-start | bytes 13762564
  12.8 1.3 copy-start.1
  73.0 72.9 %copy-start.2 = (f32[4,32,8,4,128]{4,1,3,2,0:T(8,128)S(1)}, f32[4,32,8,4,128]{4,1,3,2,0:T(8,128)}, u32[]{:S(2)}) copy-start(f32[4,32,8,4,128]{4,1,3,2,0:T(8,128)} %get-tuple-element.21) | copy-start | bytes 6291460
  74.2 0.7 copy-start.6
  110.9 2.7 %copy-start.5 = (f32[256,256]{1,0:T(8,128)}, f32[256,256]{1,0:T(8,128)S(1)}, u32[]{:S(2)}) copy-start(f32[256,256]{1,0:T(8,128)S(1)} %get-tuple-element.27) | copy-start | bytes 786436
  148.6 2.2 %copy-start.4 = (bf16[128,4096]{1,0:T(8,128)(2,1)S(1)}, bf16[128,4096]{1,0:T(8,128)(2,1)}, u32[]{:S(2)}) copy-start(bf16[128,4096]{1,0:T(8,128)(2,1)} %triangular_solve.53) | copy-start | bytes 3145732

commit v2 on v1

--- a/solution.py
+++ b/solution.py
@@ -9,51 +9,209 @@
 from jax.sharding import PartitionSpec as P
 
 MESH = pl.DeviceIdType.MESH
-
-
-def padded_2(cells, sides, width):
-    for axis, dim in sides:
-        count = lax.axis_size(axis)
-        ends = count - 1
-        head = lax.slice_in_dim(cells, 0, width, axis=dim)
-        tail = lax.slice_in_dim(cells, cells.shape[dim] - width, cells.shape[dim], axis=dim)
-        cells = jnp.concatenate(
-            [
-                lax.ppermute(tail, axis, [(i, (i + 1) % count) for i in range(ends)]),
-                cells,
-                lax.ppermute(head, axis, [((i + 1) % count, i) for i in range(ends)]),
-            ],
-            axis=dim,
-        )
-    return cells
-
-
-def derivatives(padded):
-    center = padded[:, :, 1:-1, 1:-1, 1:-1]
-    x_plus = padded[:, :, 2:, 1:-1, 1:-1]
-    x_minus = padded[:, :, :-2, 1:-1, 1:-1]
-    y_plus = padded[:, :, 1:-1, 2:, 1:-1]
-    y_minus = padded[:, :, 1:-1, :-2, 1:-1]
-    z_plus = padded[:, :, 1:-1, 1:-1, 2:]
-    z_minus = padded[:, :, 1:-1, 1:-1, :-2]
-    stacked = jnp.stack(
-        [
-            center,
-            0.5 * (x_plus - x_minus),
-            0.5 * (y_plus - y_minus),
-            0.5 * (z_plus - z_minus),
-            0.25 * (x_plus - 2.0 * center + x_minus),
-            0.25 * (y_plus - 2.0 * center + y_minus),
-            0.25 * (z_plus - 2.0 * center + z_minus),
+ROW, LANE, PANEL = 8, 128, 32
+
+
+def parts(v):
+    high = v.astype(jnp.bfloat16)
+    rest = v - high.astype(jnp.float32)
+    mid = rest.astype(jnp.bfloat16)
+    low = (rest - mid.astype(jnp.float32)).astype(jnp.bfloat16)
+    return high, mid, low
+
+
+def eliminate(rows, col0, tiles):
+    sub = lax.broadcasted_iota(jnp.int32, (ROW, LANE), 0)
+    count = len(rows)
+
+    def spread(v, q):
+        return jnp.broadcast_to(v[q:q + 1, :], (ROW, LANE))
+
+    for k in range(count):
+        lane = (col0 + ROW * k) % LANE
+        tc = tiles.index((col0 + ROW * k) // LANE)
+        cols = [
+            [jnp.broadcast_to(rows[i][tc][:, lane + q:lane + q + 1], (ROW, LANE)) for i in range(k, count)]
+            for q in range(ROW)
+        ]
+        scale = jnp.zeros((ROW, LANE), jnp.float32)
+        for q in range(ROW):
+            pivot = spread(cols[q][0], q)
+            inv = 1.0 / pivot
+            scale = jnp.where(sub == q, lax.rsqrt(pivot), scale)
+            mult = [c * inv for c in cols[q]]
+            mult[0] = jnp.where(sub > q, mult[0], 0.0)
+            for p in range(q + 1, ROW):
+                line = spread(cols[p][0], q)
+                cols[p] = [c - m * line for c, m in zip(cols[p], mult)]
+            for t in range(len(tiles)):
+                line = spread(rows[k][t], q)
+                for i, m in enumerate(mult):
+                    rows[k + i][t] = rows[k + i][t] - m * line
+        for t in range(len(tiles)):
+            rows[k][t] = rows[k][t] * scale
+    return rows
+
+
+def factor_kernel(gram_ref, feat_ref, fac_ref, out_ref, work, spread_out):
+    n = gram_ref.shape[0]
+    steps = n // PANEL
+    work[:, :n] = gram_ref[...]
+    eye_r = lax.broadcasted_iota(jnp.int32, (n, n), 0)
+    eye_c = lax.broadcasted_iota(jnp.int32, (n, n), 1)
+    work[:, n:] = jnp.where(eye_r == eye_c, 1.0, 0.0)
+    left = n // LANE
+    for p in range(steps):
+        r0 = PANEL * p
+        first = r0 // LANE
+        tiles = list(range(first, left + first + 1))
+        rows = [
+            [work[r0 + ROW * i:r0 + ROW * (i + 1), LANE * t:LANE * (t + 1)] for t in tiles]
+            for i in range(PANEL // ROW)
+        ]
+        rows = eliminate(rows, r0, tiles)
+        whole = jnp.concatenate([jnp.concatenate(r, axis=1) for r in rows], axis=0)
+        wide = LANE * (left - first)
+        upper = whole[:, :wide]
+        rr = r0 + lax.broadcasted_iota(jnp.int32, (PANEL, wide), 0)
+        cc = LANE * first + lax.broadcasted_iota(jnp.int32, (PANEL, wide), 1)
+        upper = jnp.where(cc >= rr, upper, 0.0)
+        lower = upper.T
+        fac_ref[LANE * first:, r0:r0 + PANEL] = lower
+        if first:
+            fac_ref[:LANE * first, r0:r0 + PANEL] = jnp.zeros((LANE * first, PANEL), jnp.float32)
+        work[r0:r0 + PANEL, n:n + LANE * (first + 1)] = whole[:, wide:]
+        r1 = r0 + PANEL
+        if r1 < n:
+            high, mid, low = parts(whole)
+            right = jnp.concatenate([high, high, high, mid, mid, low], axis=0)
+            lh, lm, ll = parts(lower)
+            lhs = jnp.concatenate([lh, lm, ll, lh, lm, lh], axis=1)
+            off = LANE * first
+            for s0, s1 in ((r1, r1 + PANEL), (r1 + PANEL, n)):
+                if s0 < s1:
+                    change = jnp.dot(lhs[s0 - off:s1 - off], right, preferred_element_type=jnp.float32)
+                    at = LANE * tiles[0]
+                    work[s0:s1, at:at + LANE * len(tiles)] -= change
+    inverse = work[:, n:]
+    high = inverse.astype(jnp.bfloat16)
+    mid = (inverse - high.astype(jnp.float32)).astype(jnp.bfloat16)
+    cells = feat_ref.shape[1]
+    blocks = cells // LANE
+    chunk = 4
+    for j in range(blocks // chunk):
+        x = feat_ref[:, chunk * LANE * j:chunk * LANE * (j + 1)]
+        y = jnp.dot(high, x, preferred_element_type=jnp.float32)
+        y = y + jnp.dot(mid, x, preferred_element_type=jnp.float32)
+        for b in range(chunk):
+            spread_out[pl.ds(j * chunk + b, n, stride=blocks), :] = y[:, LANE * b:LANE * (b + 1)]
+    out_ref[...] = spread_out[...].astype(jnp.bfloat16)
+
+
+def factor_and_solve(gram, features):
+    n, cells = features.shape
+    lines = n * cells // LANE
+    return pl.pallas_call(
+        factor_kernel,
+        out_shape=(
+            jax.ShapeDtypeStruct((n, n), jnp.float32),
+            jax.ShapeDtypeStruct((lines, LANE), jnp.bfloat16),
+        ),
+        in_specs=[pl.BlockSpec(memory_space=pltpu.VMEM)] * 2,
+        out_specs=(pl.BlockSpec(memory_space=pltpu.VMEM),) * 2,
+        scratch_shapes=[
+            pltpu.VMEM((n, 2 * n), jnp.float32),
+            pltpu.VMEM((lines, LANE), jnp.float32),
         ],
-        axis=1,
-    )
-    shape = stacked.shape
-    return stacked.reshape((shape[0] * shape[1],) + shape[2:])
+        compiler_params=pltpu.CompilerParams(vmem_limit_bytes=48 << 20),
+    )(gram, features)
+
+
+def spread_mix(mix, snaps, fields, rows):
+    ch, count = mix.shape
+    group = fields * snaps
+    stencils = count // fields
+    k = lax.broadcasted_iota(jnp.int32, (count, rows), 0)
+    col = lax.broadcasted_iota(jnp.int32, (count, rows), 1)
+    pick = (k // stencils == col % group // snaps) & (k % stencils == col // group)
+    pick = jnp.where(pick, 1.0, 0.0).astype(jnp.bfloat16)
+    r = lax.broadcasted_iota(jnp.int32, (snaps * ch, rows), 0)
+    c = lax.broadcasted_iota(jnp.int32, (snaps * ch, rows), 1)
+    same = r // ch == c % snaps
+    out = []
+    for part in parts(mix):
+        wide = jnp.dot(part, pick, preferred_element_type=jnp.float32)
+        wide = jnp.concatenate([wide] * snaps, axis=0)
+        out.append(jnp.where(same, wide, 0.0).astype(jnp.bfloat16))
+    return out
+
+
+def front_kernel(dims, u_ref, lo_ref, hi_ref, mix_ref, feat_ref, gram_ref, weights):
+    fields, snaps, nx, ny = dims
+    fs = fields * snaps
+    rows = 7 * fs + 8
+    h, m, l = spread_mix(mix_ref[...], snaps, fields, rows)
+    for i, w in enumerate((h, m, l, h, m, h)):
+        weights[:, rows * i:rows * (i + 1)] = w
+    lane = lax.broadcasted_iota(jnp.int32, (fs, LANE), 1)
+    zero = jnp.zeros((fs, LANE), jnp.float32)
+    pad = jnp.zeros((8, LANE), jnp.float32)
+
+    def cell(x, y):
+        if x < 0:
+            return lo_ref[pl.ds(y, fs, stride=ny), :]
+        if x >= nx:
+            return hi_ref[pl.ds(y, fs, stride=ny), :]
+        return u_ref[pl.ds(x * ny + y, fs, stride=nx * ny), :]
+
+    for x in range(nx):
+        here = [cell(x, y) for y in range(ny)]
+        columns = []
+        for y in range(ny):
+            u = here[y]
+            xp, xm = cell(x + 1, y), cell(x - 1, y)
+            yp = here[y + 1] if y + 1 < ny else zero
+            ym = here[y - 1] if y else zero
+            zp = jnp.where(lane == LANE - 1, 0.0, pltpu.roll(u, LANE - 1, 1))
+            zm = jnp.where(lane == 0, 0.0, pltpu.roll(u, 1, 1))
+            twice = 2.0 * u
+            stencil = jnp.concatenate(
+                [
+                    u,
+                    0.5 * (xp - xm), 0.5 * (yp - ym), 0.5 * (zp - zm),
+                    0.25 * (xp - twice + xm), 0.25 * (yp - twice + ym), 0.25 * (zp - twice + zm),
+                    pad,
+                ],
+                axis=0,
+            )
+            sh, sm, sl = parts(stencil)
+            columns.append(jnp.concatenate([sh, sh, sh, sm, sm, sl], axis=0))
+        right = jnp.concatenate(columns, axis=1)
+        out = jnp.dot(weights[...], right, preferred_element_type=jnp.float32)
+        feat_ref[:, ny * LANE * x:ny * LANE * (x + 1)] = out.astype(jnp.bfloat16)
+    f = feat_ref[...]
+    gram_ref[...] = lax.dot_general(f, f, (((1,), (1,)), ((), ())), preferred_element_type=jnp.float32)
+
+
+def front(fields, lo, hi, mix):
+    nf, ns, nx, ny, nz = fields.shape
+    width = ns * mix.shape[0]
+    rows = 7 * nf * ns + 8
+    return pl.pallas_call(
+        functools.partial(front_kernel, (nf, ns, nx, ny)),
+        out_shape=(
+            jax.ShapeDtypeStruct((width, nx * ny * nz), jnp.bfloat16),
+            jax.ShapeDtypeStruct((width, width), jnp.float32),
+        ),
+        in_specs=[pl.BlockSpec(memory_space=pltpu.VMEM)] * 4,
+        out_specs=(pl.BlockSpec(memory_space=pltpu.VMEM),) * 2,
+        scratch_shapes=[pltpu.VMEM((width, 6 * rows), jnp.bfloat16)],
+        compiler_params=pltpu.CompilerParams(vmem_limit_bytes=48 << 20),
+    )(fields.reshape(-1, nz), lo.reshape(-1, nz), hi.reshape(-1, nz), mix)
 
 
 def running_kernel(
-    side, steps, gram_ref, out_ref,
+    side, steps, cells, gram_ref, out_ref,
     stack, pair_in, mine, got_a, got_b, got_y, whole,
     pair_send, pair_recv, a_send, a_recv, b_send, b_recv,
     y_send, y_recv, g_send, g_recv, f_send, f_recv,
@@ -155,6 +313,9 @@
         def _():
             whole[core, a] += got_y[k]
 
+    count = (t + 1).astype(jnp.float32) * jnp.float32(cells)
+    whole[core, a] = whole[core, a] / count
+
     def forward(k):
         return copy(whole.at[core, k], whole.at[core, k], f_send.at[k], f_recv.at[k], partner)
 
@@ -195,7 +356,7 @@
             copy(got_y.at[t], got_y.at[t], y_send.at[d], y_recv.at[t], at_t(k)).wait_send()
 
 
-def running_sum(gram):
+def running_mean(gram, cells):
     side = math.isqrt(lax.axis_size("rows") // 2)
     steps = lax.axis_size("tm")
     width = gram.shape[0]
@@ -205,7 +366,7 @@
     dma = pltpu.SemaphoreType.DMA
     f32 = jnp.float32
     return pl.pallas_call(
-        functools.partial(running_kernel, side, steps),
+        functools.partial(running_kernel, side, steps, cells * lax.axis_size("rows")),
         out_shape=jax.ShapeDtypeStruct((width, width), f32),
         in_specs=[pl.BlockSpec(memory_space=pltpu.VMEM)],
         out_specs=pl.BlockSpec(memory_space=pltpu.VMEM),
@@ -229,27 +390,15 @@
 
 
 def body(fields, channel_mix):
-    grown = padded_2(fields, (("rows", 2),), 1)
-    padded = jnp.pad(grown, ((0, 0), (0, 0), (0, 0), (1, 1), (1, 1)))
-    stencil = derivatives(padded)
-    channels = jnp.einsum(
-        "ck,ksxyz->scxyz", channel_mix, stencil, precision=lax.Precision.HIGHEST
-    ).astype(jnp.bfloat16)
-    width = channels.shape[0] * channels.shape[1]
-    local_cells = channels.shape[2] * channels.shape[3] * channels.shape[4]
-    features = channels.reshape(width, local_cells)
-    gram = lax.dot_general(
-        features, features, (((1,), (1,)), ((), ())), preferred_element_type=jnp.float32
-    )
-    running_gram = running_sum(gram)
-    row_count = (lax.axis_index("tm") + 1).astype(jnp.float32) * jnp.float32(
-        local_cells * lax.axis_size("rows")
-    )
-    factor = lax.linalg.cholesky(running_gram / row_count, symmetrize_input=False)
-    solved = lax.linalg.triangular_solve(
-        factor, features.astype(jnp.float32), left_side=True, lower=True
-    )
-    coefficients = solved.reshape(channels.shape).astype(jnp.bfloat16)
+    count = lax.axis_size("rows")
+    up = [(i, i + 1) for i in range(count - 1)]
+    down = [(i + 1, i) for i in range(count - 1)]
+    lo = lax.ppermute(fields[:, :, -1:], "rows", up)
+    hi = lax.ppermute(fields[:, :, :1], "rows", down)
+    features, gram = front(fields, lo, hi, channel_mix)
+    factor, solved = factor_and_solve(running_mean(gram, features.shape[1]), features)
+    _, snaps, nx, ny, nz = fields.shape
+    coefficients = solved.reshape(snaps, channel_mix.shape[0], nx, ny, nz)
     return (factor[None], coefficients)
 
 

time: 160 us -> 76.4 us (0.48)
  other arithmetic: 64.8 us -> 0 us
  local copies, waits for them, and re-layouts: 28.2 us -> 4.39 us
  Pallas kernels: 42.6 us -> 63.9 us
  matrix products: 15.2 us -> 0 us
    another operation x12 -> x0, other arithmetic: 60.3 us -> none  [the longest x6 35.2 us: body(): lax.linalg.cholesky(running_gram / row_count, symmetrize_input=False)]
    pallas_call x1 -> x3, Pallas kernels: 42.6 us -> 63.9 us  [the longest x1 45.4 us: running_mean(): pl.pallas_call(functools.partial(running_kernel, side, steps, cells * lax...]
    another operation x13 -> x0, local copies, waits for them, and re-layouts: 15 us -> none  [the longest x5 9.74 us: body(): lax.linalg.triangular_solve(factor, features.astype(jnp.float32), left_si...]
    dot_general x2 -> x0, matrix products: 8.12 us -> none  [the longest x1 6.68 us: body(): jnp.einsum('ck,ksxyz->scxyz', channel_mix, stencil, precision=lax.Precisi...]
    another operation x5 -> x0, matrix products: 7.1 us -> none  [the longest x3 4.94 us: body(): lax.linalg.triangular_solve(factor, features.astype(jnp.float32), left_si...]
    convert_element_type x2 -> x0, local copies, waits for them, and re-layouts: 5.11 us -> none  [the longest x1 2.71 us: body(): coefficients = solved.reshape(channels.shape).astype(jnp.bfloat16)]
    reshape x1 -> x0, local copies, waits for them, and re-layouts: 3.29 us -> none  [body(): features = channels.reshape(width, local_cells)]
    concatenate x1 -> x0, other arithmetic: 1.79 us -> none  [padded_2(): jnp.concatenate([lax.ppermute(tail, axis, [(i, (i + 1) % count) for i in...]
  transfers between devices with their start and end apart: 2 -> 2, of which waited for: 0 -> 2; matrix products, arithmetic and copies ran while one was open for 2% -> 0% of each run, Pallas kernels for 0% -> 0%
where the time goes in v2:
time: 76.4 us; the launch traced here: 76 us
  Pallas kernels  63.9 us (84%)
  starting transfers between devices  5.6 us (7%)
  local copies, waits for them, and re-layouts  4.39 us (6%)
  waiting for transfers between devices  1.46 us (2%)
    pallas_call x1, Pallas kernels, running_mean(): pl.pallas_call(functools.partial(running_kernel, side, steps, cells * lax...  45.4 us
    pallas_call x1, Pallas kernels, factor_and_solve(): pl.pallas_call(factor_kernel, out_shape=(jax.ShapeDtypeStruct((n, n), jnp...  13.1 us
    pallas_call x1, Pallas kernels, front(): pl.pallas_call(functools.partial(front_kernel, (nf, ns, nx, ny)), out_sha...  5.36 us
    unnamed x8, local copies, waits for them, and re-layouts  3.44 us
    ppermute x1, starting transfers between devices, body(): lo = lax.ppermute(fields[:, :, -1:], 'rows', up)  3.02 us
    ppermute x1, starting transfers between devices, body(): hi = lax.ppermute(fields[:, :, :1], 'rows', down)  2.58 us
  transfers between devices with their start and end apart: 2, of which 2 were waited for; matrix products, arithmetic and copies ran while one was open for 0% of the time, Pallas kernels for 0%

profile of v2, /device:TPU:113, one launch (start us, length us, event | category | flops | bytes accessed | tf_op | source)
XLA Modules:
  0.0 76.0 jit_solution(11416492343611727955)
XLA Ops:
  0.6 0.9 %fusion = (f32[5,8,1,4,128]{4,3,2,1,0:T(4,128)S(1)}, f32[5,8,1,4,128]{4,3,2,1,0:T(4,128)S(1)}) fusion(f32[5,8,8,4,128]{4,3,2,1,0:T(4,128)} %param.2), kind=kLoop, calls=%fused_computation | loop fusion | bytes 327680 | tf_op jit(solution)/shard_map/slice | solution.py:397
  1.6 2.6 %collective-permute-start.1 = (f32[5,8,1,4,128]{4,3,2,1,0:T(4,128)S(1)}, f32[5,8,1,4,128]{4,3,2,1,0:T(4,128)S(1)}, u32[]{:S(2)}, u32[]{:S(2)}) collective-permute-start(f32[5,8,1,4,128]{4,3,2,1,0:T(4,128)S(1)} %get-tuple-element.10), channel_id=1, source_target_pairs={{8,0},{16,8},{24,16},{32,24},{40,32},{48,40},{56,48},{64,56},{72,6... | collective-permute-start | bytes 245768 | tf_op jit(solution)/shard_map/ppermute | solution.py:397
  4.2 3.0 %collective-permute-start = (f32[5,8,1,4,128]{4,3,2,1,0:T(4,128)S(1)}, f32[5,8,1,4,128]{4,3,2,1,0:T(4,128)S(1)}, u32[]{:S(2)}, u32[]{:S(2)}) collective-permute-start(f32[5,8,1,4,128]{4,3,2,1,0:T(4,128)S(1)} %get-tuple-element.11), channel_id=1, source_target_pairs={{0,8},{8,16},{16,24},{24,32},{32,40},{40,48},{48,56},{56,64},{64,7... | collective-permute-start | bytes 245768 | tf_op jit(solution)/shard_map/ppermute | solution.py:396
  7.2 0.2 collective-permute-done.1
  7.4 1.3 %collective-permute-done = f32[5,8,1,4,128]{4,3,2,1,0:T(4,128)S(1)} collective-permute-done((f32[5,8,1,4,128]{4,3,2,1,0:T(4,128)S(1)}, f32[5,8,1,4,128]{4,3,2,1,0:T(4,128)S(1)}, u32[]{:S(2)}, u32[]{:S(2)}) %collective-permute-start) | collective-permute-done | bytes 81952 | tf_op jit(solution)/shard_map/ppermute | solution.py:396
  8.7 0.0 copy-start.1
  8.7 1.1 %copy-done.1 = f32[5,8,8,4,128]{4,3,2,1,0:T(4,128)S(1)} copy-done((f32[5,8,8,4,128]{4,3,2,1,0:T(4,128)S(1)}, f32[5,8,8,4,128]{4,3,2,1,0:T(4,128)}, u32[]{:S(2)}) %copy-start.1) | copy-done | bytes 655384
  9.7 0.0 copy-start.3
  9.7 0.7 copy-done.3
  10.5 5.4 %shard_map.41 = (bf16[256,4096]{1,0:T(8,128)(2,1)S(1)}, f32[256,256]{1,0:T(8,128)S(1)}) custom-call(f32[1280,128]{1,0:T(8,128)S(1)} %bitcast.5, f32[160,128]{1,0:T(8,128)S(1)} %bitcast.7, f32[160,128]{1,0:T(8,128)S(1)} %bitcast.6, f32[32,35]{1,0:T(8,128)S(1)} %copy-done.3), custom_call_target="tpu_custom_call" | custom-call | tf_op jit(solution)/shard_map/pallas_call | solution.py:200
  15.8 0.0 copy-start.2
  15.8 0.7 copy-done.2
  16.5 45.4 %shard_map.42.gram_ref = f32[256,256]{1,0:T(8,128)} custom-call(f32[256,256]{1,0:T(8,128)} %copy-done.2), custom_call_target="tpu_custom_call" | custom-call | tf_op jit(solution)/shard_map/pallas_call | solution.py:368
  62.0 0.0 copy-start
  62.0 0.9 %copy-done = f32[256,256]{1,0:T(8,128)S(1)} copy-done((f32[256,256]{1,0:T(8,128)S(1)}, f32[256,256]{1,0:T(8,128)}, u32[]{:S(2)}) %copy-start) | copy-done | bytes 262168
  62.9 13.1 %shard_map.43 = (f32[256,256]{1,0:T(8,128)}, bf16[8192,128]{1,0:T(8,128)(2,1)}) custom-call(f32[256,256]{1,0:T(8,128)S(1)} %copy-done, bf16[256,4096]{1,0:T(8,128)(2,1)S(1)} %get-tuple-element.7.feat_ref), custom_call_target="tpu_custom_call" | custom-call | tf_op jit(solution)/shard_map/pallas_call | solution.py:114
Async XLA Ops:
  1.6 5.8 %collective-permute-start.1 = (f32[5,8,1,4,128]{4,3,2,1,0:T(4,128)S(1)}, f32[5,8,1,4,128]{4,3,2,1,0:T(4,128)S(1)}, u32[]{:S(2)}, u32[]{:S(2)}) collective-permute-start(f32[5,8,1,4,128]{4,3,2,1,0:T(4,128)S(1)} %get-tuple-element.10), channel_id=1, source_target_pairs={{8,0},{16,8},{24,16},{32,24},{40,32},{48,40},{56,48},{64,56},{72,6... | collective-permute-start | bytes 245768 | tf_op jit(solution)/shard_map/ppermute | solution.py:397
  4.2 4.5 %collective-permute-start = (f32[5,8,1,4,128]{4,3,2,1,0:T(4,128)S(1)}, f32[5,8,1,4,128]{4,3,2,1,0:T(4,128)S(1)}, u32[]{:S(2)}, u32[]{:S(2)}) collective-permute-start(f32[5,8,1,4,128]{4,3,2,1,0:T(4,128)S(1)} %get-tuple-element.11), channel_id=1, source_target_pairs={{0,8},{8,16},{16,24},{24,32},{32,40},{40,48},{48,56},{56,64},{64,7... | collective-permute-start | bytes 245768 | tf_op jit(solution)/shard_map/ppermute | solution.py:396
  8.7 1.1 %copy-start.1 = (f32[5,8,8,4,128]{4,3,2,1,0:T(4,128)S(1)}, f32[5,8,8,4,128]{4,3,2,1,0:T(4,128)}, u32[]{:S(2)}) copy-start(f32[5,8,8,4,128]{4,3,2,1,0:T(4,128)} %param.2) | copy-start | bytes 1966084
  9.7 0.7 copy-start.3
  15.8 0.7 copy-start.2
  62.0 1.0 %copy-start = (f32[256,256]{1,0:T(8,128)S(1)}, f32[256,256]{1,0:T(8,128)}, u32[]{:S(2)}) copy-start(f32[256,256]{1,0:T(8,128)} %shard_map.42.gram_ref) | copy-start | bytes 786436

commit v3 on v2

--- a/solution.py
+++ b/solution.py
@@ -146,32 +146,92 @@
     return out
 
 
-def front_kernel(dims, u_ref, lo_ref, hi_ref, mix_ref, feat_ref, gram_ref, weights):
+def gram_kernel(
+    dims, side, steps, count, u_hbm, mix_ref, feat_hbm, out_ref,
+    u_ref, feat, weights, to_left, to_right, lo, hi,
+    stack, pair_in, mine, got_a, got_b, got_y, whole,
+    u_sem, feat_sem, l_send, l_recv, r_send, r_recv,
+    pair_send, pair_recv, a_send, a_recv, b_send, b_recv,
+    y_send, y_recv, g_send, g_recv, f_send, f_recv,
+):
     fields, snaps, nx, ny = dims
     fs = fields * snaps
+    load = pltpu.make_async_copy(u_hbm, u_ref, u_sem)
+    load.start()
+    here = lax.axis_index("rows")
+    t = lax.axis_index("tm")
+    size = 2 * side * side
+    core = here % 2
+    chip = here // 2
+    z, x = chip // side, chip % side
+    a = (1 - core) * x + core * z
+    b = (1 - core) * z + core * x
+    a_step = (1 - core) + core * side
+    b_step = (1 - core) * side + core
+    half = stack.shape[1]
+    piece = half // side
+
+    def at_a(k):
+        return {"rows": 2 * (k * a_step + b * b_step) + core}
+
+    def at_b(k):
+        return {"rows": 2 * (a * a_step + k * b_step) + core}
+
+    def at_t(k):
+        return {"tm": k}
+
+    partner = {"rows": 2 * chip + 1 - core}
+
+    def copy(src, dst, send, recv, to):
+        return pltpu.make_async_remote_copy(
+            src_ref=src, dst_ref=dst, send_sem=send, recv_sem=recv,
+            device_id=to, device_id_type=MESH,
+        )
+
+    left = {"rows": (here + size - 1) % size}
+    right = {"rows": (here + 1) % size}
+    barrier = pltpu.get_barrier_semaphore()
+    for near in (left, right, partner):
+        pl.semaphore_signal(barrier, inc=1, device_id=near, device_id_type=MESH)
+    for d in range(1, side):
+        pl.semaphore_signal(barrier, inc=1, device_id=at_a((a + d) % side), device_id_type=MESH)
+        pl.semaphore_signal(barrier, inc=1, device_id=at_b((b + d) % side), device_id_type=MESH)
+    for d in range(1, steps):
+        pl.semaphore_signal(barrier, inc=1, device_id=at_t((t + d) % steps), device_id_type=MESH)
+
     rows = 7 * fs + 8
     h, m, l = spread_mix(mix_ref[...], snaps, fields, rows)
     for i, w in enumerate((h, m, l, h, m, h)):
         weights[:, rows * i:rows * (i + 1)] = w
+
+    def at(x, y):
+        return u_ref[pl.ds(x * ny + y, fs, stride=nx * ny), :]
+
+    load.wait()
+    for y in range(ny):
+        to_left[fs * y:fs * (y + 1), :] = at(0, y)
+        to_right[fs * y:fs * (y + 1), :] = at(nx - 1, y)
+
+    pl.semaphore_wait(barrier, 2 * (side - 1) + steps + 2)
+
+    go_left = copy(to_left, hi, l_send, l_recv, left)
+    go_right = copy(to_right, lo, r_send, r_recv, right)
+    go_left.start()
+    go_right.start()
+    sends = [go_left, go_right]
+
     lane = lax.broadcasted_iota(jnp.int32, (fs, LANE), 1)
     zero = jnp.zeros((fs, LANE), jnp.float32)
     pad = jnp.zeros((8, LANE), jnp.float32)
 
-    def cell(x, y):
-        if x < 0:
-            return lo_ref[pl.ds(y, fs, stride=ny), :]
-        if x >= nx:
-            return hi_ref[pl.ds(y, fs, stride=ny), :]
-        return u_ref[pl.ds(x * ny + y, fs, stride=nx * ny), :]
-
-    for x in range(nx):
-        here = [cell(x, y) for y in range(ny)]
+    def plane(x, before, after):
+        mid = [at(x, y) for y in range(ny)]
         columns = []
         for y in range(ny):
-            u = here[y]
-            xp, xm = cell(x + 1, y), cell(x - 1, y)
-            yp = here[y + 1] if y + 1 < ny else zero
-            ym = here[y - 1] if y else zero
+            u = mid[y]
+            xp, xm = after(y), before(y)
+            yp = mid[y + 1] if y + 1 < ny else zero
+            ym = mid[y - 1] if y else zero
             zp = jnp.where(lane == LANE - 1, 0.0, pltpu.roll(u, LANE - 1, 1))
             zm = jnp.where(lane == 0, 0.0, pltpu.roll(u, 1, 1))
             twice = 2.0 * u
@@ -186,84 +246,36 @@
             )
             sh, sm, sl = parts(stencil)
             columns.append(jnp.concatenate([sh, sh, sh, sm, sm, sl], axis=0))
-        right = jnp.concatenate(columns, axis=1)
-        out = jnp.dot(weights[...], right, preferred_element_type=jnp.float32)
-        feat_ref[:, ny * LANE * x:ny * LANE * (x + 1)] = out.astype(jnp.bfloat16)
-    f = feat_ref[...]
-    gram_ref[...] = lax.dot_general(f, f, (((1,), (1,)), ((), ())), preferred_element_type=jnp.float32)
-
-
-def front(fields, lo, hi, mix):
-    nf, ns, nx, ny, nz = fields.shape
-    width = ns * mix.shape[0]
-    rows = 7 * nf * ns + 8
-    return pl.pallas_call(
-        functools.partial(front_kernel, (nf, ns, nx, ny)),
-        out_shape=(
-            jax.ShapeDtypeStruct((width, nx * ny * nz), jnp.bfloat16),
-            jax.ShapeDtypeStruct((width, width), jnp.float32),
-        ),
-        in_specs=[pl.BlockSpec(memory_space=pltpu.VMEM)] * 4,
-        out_specs=(pl.BlockSpec(memory_space=pltpu.VMEM),) * 2,
-        scratch_shapes=[pltpu.VMEM((width, 6 * rows), jnp.bfloat16)],
-        compiler_params=pltpu.CompilerParams(vmem_limit_bytes=48 << 20),
-    )(fields.reshape(-1, nz), lo.reshape(-1, nz), hi.reshape(-1, nz), mix)
-
-
-def running_kernel(
-    side, steps, cells, gram_ref, out_ref,
-    stack, pair_in, mine, got_a, got_b, got_y, whole,
-    pair_send, pair_recv, a_send, a_recv, b_send, b_recv,
-    y_send, y_recv, g_send, g_recv, f_send, f_recv,
-):
-    here = lax.axis_index("rows")
-    t = lax.axis_index("tm")
-    core = here % 2
-    chip = here // 2
-    z, x = chip // side, chip % side
-    a = (1 - core) * x + core * z
-    b = (1 - core) * z + core * x
-    a_step = (1 - core) + core * side
-    b_step = (1 - core) * side + core
-    half = stack.shape[1]
-    piece = half // side
-
-    def at_a(k):
-        return {"rows": 2 * (k * a_step + b * b_step) + core}
-
-    def at_b(k):
-        return {"rows": 2 * (a * a_step + k * b_step) + core}
-
-    def at_t(k):
-        return {"tm": k}
-
-    partner = {"rows": 2 * chip + 1 - core}
-
-    def copy(src, dst, send, recv, to):
-        return pltpu.make_async_remote_copy(
-            src_ref=src, dst_ref=dst, send_sem=send, recv_sem=recv,
-            device_id=to, device_id_type=MESH,
-        )
-
-    barrier = pltpu.get_barrier_semaphore()
-    pl.semaphore_signal(barrier, inc=1, device_id=partner, device_id_type=MESH)
-    for d in range(1, side):
-        pl.semaphore_signal(barrier, inc=1, device_id=at_a((a + d) % side), device_id_type=MESH)
-        pl.semaphore_signal(barrier, inc=1, device_id=at_b((b + d) % side), device_id_type=MESH)
-    for d in range(1, steps):
-        pl.semaphore_signal(barrier, inc=1, device_id=at_t((t + d) % steps), device_id_type=MESH)
-
-    edge = gram_ref.shape[0] // 2
-    flat = [gram_ref[:edge, :edge], gram_ref[edge:, :edge], gram_ref[edge:, edge:]]
+        values = jnp.dot(weights[...], jnp.concatenate(columns, axis=1), preferred_element_type=jnp.float32)
+        feat[:, ny * LANE * x:ny * LANE * (x + 1)] = values.astype(jnp.bfloat16)
+
+    for x in range(1, nx - 1):
+        plane(x, lambda y: at(x - 1, y), lambda y: at(x + 1, y))
+
+    go_right.wait_recv()
+    plane(
+        0,
+        lambda y: jnp.where(here > 0, lo[fs * y:fs * (y + 1), :], 0.0),
+        lambda y: at(1, y),
+    )
+    go_left.wait_recv()
+    plane(
+        nx - 1,
+        lambda y: at(nx - 2, y),
+        lambda y: jnp.where(here < size - 1, hi[fs * y:fs * (y + 1), :], 0.0),
+    )
+
+    keep = pltpu.make_async_copy(feat, feat_hbm, feat_sem)
+    keep.start()
+    edge = out_ref.shape[0] // 2
     cut = edge // 2
-    stack[0, :edge] = flat[0]
-    stack[0, edge:] = flat[1][:cut]
-    stack[1, :cut] = flat[1][cut:]
-    stack[1, cut:] = flat[2]
-
-    pl.semaphore_wait(barrier, 2 * (side - 1) + steps)
-
-    sends = []
+    f = feat[...]
+    gram = lax.dot_general(f, f, (((1,), (1,)), ((), ())), preferred_element_type=jnp.float32)
+    stack[0, :edge] = gram[:edge, :edge]
+    stack[0, edge:] = gram[edge:edge + cut, :edge]
+    stack[1, :cut] = gram[edge + cut:, :edge]
+    stack[1, cut:] = gram[edge:, edge:]
+
     pair = copy(stack.at[1 - core], pair_in, pair_send, pair_recv, partner)
     pair.start()
     sends.append(pair)
@@ -313,8 +325,7 @@
         def _():
             whole[core, a] += got_y[k]
 
-    count = (t + 1).astype(jnp.float32) * jnp.float32(cells)
-    whole[core, a] = whole[core, a] / count
+    whole[core, a] = whole[core, a] / ((t + 1).astype(jnp.float32) * jnp.float32(count))
 
     def forward(k):
         return copy(whole.at[core, k], whole.at[core, k], f_send.at[k], f_recv.at[k], partner)
@@ -354,23 +365,35 @@
         @pl.when(k < steps)
         def _():
             copy(got_y.at[t], got_y.at[t], y_send.at[d], y_recv.at[t], at_t(k)).wait_send()
-
-
-def running_mean(gram, cells):
+    keep.wait()
+
+
+def features_and_mean(fields, mix):
+    nf, ns, nx, ny, nz = fields.shape
     side = math.isqrt(lax.axis_size("rows") // 2)
     steps = lax.axis_size("tm")
-    width = gram.shape[0]
+    width = ns * mix.shape[0]
+    cells = nx * ny * nz
+    rows = 7 * nf * ns + 8
     edge = width // 2
     half = 3 * edge // 2
     piece = half // side
+    plane = nf * ns * ny
     dma = pltpu.SemaphoreType.DMA
-    f32 = jnp.float32
+    f32, bf16 = jnp.float32, jnp.bfloat16
     return pl.pallas_call(
-        functools.partial(running_kernel, side, steps, cells * lax.axis_size("rows")),
-        out_shape=jax.ShapeDtypeStruct((width, width), f32),
-        in_specs=[pl.BlockSpec(memory_space=pltpu.VMEM)],
-        out_specs=pl.BlockSpec(memory_space=pltpu.VMEM),
+        functools.partial(gram_kernel, (nf, ns, nx, ny), side, steps, cells * lax.axis_size("rows")),
+        out_shape=(jax.ShapeDtypeStruct((width, cells), bf16), jax.ShapeDtypeStruct((width, width), f32)),
+        in_specs=[pl.BlockSpec(memory_space=pl.ANY), pl.BlockSpec(memory_space=pltpu.VMEM)],
+        out_specs=(pl.BlockSpec(memory_space=pl.ANY), pl.BlockSpec(memory_space=pltpu.VMEM)),
         scratch_shapes=[
+            pltpu.VMEM((nf * ns * nx * ny, nz), f32),
+            pltpu.VMEM((width, cells), bf16),
+            pltpu.VMEM((width, 6 * rows), bf16),
+            pltpu.VMEM((plane, nz), f32),
+            pltpu.VMEM((plane, nz), f32),
+            pltpu.VMEM((plane, nz), f32),
+            pltpu.VMEM((plane, nz), f32),
             pltpu.VMEM((2, half, edge), f32),
             pltpu.VMEM((half, edge), f32),
             pltpu.VMEM((side, piece, edge), f32),
@@ -378,6 +401,7 @@
             pltpu.VMEM((side, piece, edge), f32),
             pltpu.VMEM((steps, piece, edge), f32),
             pltpu.VMEM((2, side, piece, edge), f32),
+            dma, dma, dma, dma, dma, dma,
             dma, dma,
             dma((side,)), dma((side,)),
             dma((side,)), dma((side,)),
@@ -385,18 +409,15 @@
             dma((side,)), dma((side,)),
             dma((side,)), dma((side,)),
         ],
-        compiler_params=pltpu.CompilerParams(collective_id=0, has_side_effects=True),
-    )(gram)
+        compiler_params=pltpu.CompilerParams(
+            collective_id=0, has_side_effects=True, vmem_limit_bytes=56 << 20
+        ),
+    )(fields.reshape(-1, nz), mix)
 
 
 def body(fields, channel_mix):
-    count = lax.axis_size("rows")
-    up = [(i, i + 1) for i in range(count - 1)]
-    down = [(i + 1, i) for i in range(count - 1)]
-    lo = lax.ppermute(fields[:, :, -1:], "rows", up)
-    hi = lax.ppermute(fields[:, :, :1], "rows", down)
-    features, gram = front(fields, lo, hi, channel_mix)
-    factor, solved = factor_and_solve(running_mean(gram, features.shape[1]), features)
+    features, mean = features_and_mean(fields, channel_mix)
+    factor, solved = factor_and_solve(mean, features)
     _, snaps, nx, ny, nz = fields.shape
     coefficients = solved.reshape(snaps, channel_mix.shape[0], nx, ny, nz)
     return (factor[None], coefficients)

time: 76.4 us -> 66.6 us (0.87)
  starting transfers between devices: 5.6 us -> 0 us
  local copies, waits for them, and re-layouts: 4.39 us -> 2.53 us
  waiting for transfers between devices: 1.46 us -> 0 us
    ppermute x2 -> x0, starting transfers between devices: 5.6 us -> none  [the longest x1 3.02 us: body(): lo = lax.ppermute(fields[:, :, -1:], 'rows', up)]
    ppermute x2 -> x0, waiting for transfers between devices: 1.46 us -> none  [the longest x1 1.28 us: body(): lo = lax.ppermute(fields[:, :, -1:], 'rows', up)]
    slice x1 -> x0, local copies, waits for them, and re-layouts: 0.94 us -> none  [body(): hi = lax.ppermute(fields[:, :, :1], 'rows', down)]
    unnamed x8 -> x4, local copies, waits for them, and re-layouts: 3.44 us -> 2.53 us
    pallas_call x2 -> x1, Pallas kernels: 50.8 us -> 50.1 us  [features_and_mean(): pl.pallas_call(functools.partial(gram_kernel, (nf, ns, nx, ny), side, ste...]
  transfers between devices with their start and end apart: 2 -> 0, of which waited for: 2 -> 0; matrix products, arithmetic and copies ran while one was open for 0% -> 0% of each run, Pallas kernels for 0% -> 0%
where the time goes in v3:
time: 66.6 us; the launch traced here: 66.3 us
  Pallas kernels  63.2 us (95%)
  local copies, waits for them, and re-layouts  2.53 us (4%)
    pallas_call x1, Pallas kernels, features_and_mean(): pl.pallas_call(functools.partial(gram_kernel, (nf, ns, nx, ny), side, ste...  50.1 us
    pallas_call x1, Pallas kernels, factor_and_solve(): pl.pallas_call(factor_kernel, out_shape=(jax.ShapeDtypeStruct((n, n), jnp...  13.1 us
    unnamed x4, local copies, waits for them, and re-layouts  2.53 us

profile of v3, /device:TPU:113, one launch (start us, length us, event | category | flops | bytes accessed | tf_op | source)
XLA Modules:
  0.0 66.3 jit_solution(7707953920805748927)
XLA Ops:
  0.6 50.1 %shard_map.41 = (bf16[256,4096]{1,0:T(8,128)(2,1)}, f32[256,256]{1,0:T(8,128)}) custom-call(f32[1280,128]{1,0:T(8,128)} %bitcast.3, f32[32,35]{1,0:T(8,128)} %mix_ref.1), custom_call_target="tpu_custom_call" | custom-call | tf_op jit(solution)/shard_map/pallas_call | solution.py:384
  50.7 0.0 copy-start
  50.7 1.6 %copy-done = bf16[256,4096]{1,0:T(8,128)(2,1)S(1)} copy-done((bf16[256,4096]{1,0:T(8,128)(2,1)S(1)}, bf16[256,4096]{1,0:T(8,128)(2,1)}, u32[]{:S(2)}) %copy-start) | copy-done | bytes 2097176
  52.3 0.0 copy-start.1
  52.3 0.9 %copy-done.1 = f32[256,256]{1,0:T(8,128)S(1)} copy-done((f32[256,256]{1,0:T(8,128)S(1)}, f32[256,256]{1,0:T(8,128)}, u32[]{:S(2)}) %copy-start.1) | copy-done | bytes 262168
  53.3 13.1 %shard_map.42 = (f32[256,256]{1,0:T(8,128)}, bf16[8192,128]{1,0:T(8,128)(2,1)}) custom-call(f32[256,256]{1,0:T(8,128)S(1)} %copy-done.1, bf16[256,4096]{1,0:T(8,128)(2,1)S(1)} %copy-done), custom_call_target="tpu_custom_call" | custom-call | tf_op jit(solution)/shard_map/pallas_call | solution.py:114
Async XLA Ops:
  50.7 1.6 %copy-start = (bf16[256,4096]{1,0:T(8,128)(2,1)S(1)}, bf16[256,4096]{1,0:T(8,128)(2,1)}, u32[]{:S(2)}) copy-start(bf16[256,4096]{1,0:T(8,128)(2,1)} %get-tuple-element.7.feat_ref) | copy-start | bytes 6291460
  52.3 0.9 %copy-start.1 = (f32[256,256]{1,0:T(8,128)S(1)}, f32[256,256]{1,0:T(8,128)}, u32[]{:S(2)}) copy-start(f32[256,256]{1,0:T(8,128)} %get-tuple-element.6.gram_ref) | copy-start | bytes 786436

commit v4 on v3

--- a/solution.py
+++ b/solution.py
@@ -10,6 +10,7 @@
 
 MESH = pl.DeviceIdType.MESH
 ROW, LANE, PANEL = 8, 128, 32
+PITCH = 40
 
 
 def parts(v):
@@ -35,32 +36,82 @@
             for q in range(ROW)
         ]
         scale = jnp.zeros((ROW, LANE), jnp.float32)
-        for q in range(ROW):
-            pivot = spread(cols[q][0], q)
-            inv = 1.0 / pivot
-            scale = jnp.where(sub == q, lax.rsqrt(pivot), scale)
-            mult = [c * inv for c in cols[q]]
-            mult[0] = jnp.where(sub > q, mult[0], 0.0)
-            for p in range(q + 1, ROW):
-                line = spread(cols[p][0], q)
-                cols[p] = [c - m * line for c, m in zip(cols[p], mult)]
+        for q in range(0, ROW, 2):
+            p0, cross, p1 = spread(cols[q][0], q), spread(cols[q][0], q + 1), spread(cols[q + 1][0], q + 1)
+            det = p0 * p1 - cross * cross
+            inv0 = 1.0 / p0
+            inv1 = p0 * (1.0 / det)
+            ratio = cross * inv0
+            scale = jnp.where(sub == q, lax.rsqrt(p0), scale)
+            scale = jnp.where(sub == q + 1, lax.rsqrt(det * inv0), scale)
+            m0 = [c * inv0 for c in cols[q]]
+            m0[0] = jnp.where(sub > q, m0[0], 0.0)
+            m1 = [(c - m * cross) * inv1 for c, m in zip(cols[q + 1], m0)]
+            m1[0] = jnp.where(sub > q + 1, m1[0], 0.0)
+            for p in range(q + 2, ROW):
+                line0 = spread(cols[p][0], q)
+                line1 = spread(cols[p][0], q + 1) - ratio * line0
+                cols[p] = [(c - a * line0) - b * line1 for c, a, b in zip(cols[p], m0, m1)]
             for t in range(len(tiles)):
-                line = spread(rows[k][t], q)
-                for i, m in enumerate(mult):
-                    rows[k + i][t] = rows[k + i][t] - m * line
+                line0 = spread(rows[k][t], q)
+                line1 = spread(rows[k][t], q + 1) - ratio * line0
+                for i in range(len(m0)):
+                    rows[k + i][t] = (rows[k + i][t] - m0[i] * line0) - m1[i] * line1
         for t in range(len(tiles)):
             rows[k][t] = rows[k][t] * scale
     return rows
 
 
-def factor_kernel(gram_ref, feat_ref, fac_ref, out_ref, work, spread_out):
-    n = gram_ref.shape[0]
+def factor_kernel(
+    mean_hbm, feat_hbm, fac_ref, out_hbm, mean, work, feat, spread_out, packed, mean_sem, feat_sem, out_sems
+):
+    n = work.shape[0]
     steps = n // PANEL
-    work[:, :n] = gram_ref[...]
+    top = n // 2
+    load = pltpu.make_async_copy(mean_hbm, mean, mean_sem)
+    load.start()
+    fetch = pltpu.make_async_copy(feat_hbm, feat, feat_sem)
+    fetch.start()
     eye_r = lax.broadcasted_iota(jnp.int32, (n, n), 0)
     eye_c = lax.broadcasted_iota(jnp.int32, (n, n), 1)
     work[:, n:] = jnp.where(eye_r == eye_c, 1.0, 0.0)
     left = n // LANE
+    blocks = feat.shape[1] // LANE
+    stores = []
+
+    def apply(r0, r1, depth):
+        count = r1 - r0
+        inverse = work[r0:r1, n:n + depth]
+        high = inverse.astype(jnp.bfloat16)
+        mid = (inverse - high.astype(jnp.float32)).astype(jnp.bfloat16)
+        both = jnp.concatenate([high, mid], axis=0)
+        chunk = 4
+        for j in range(blocks // chunk):
+            x = feat[:depth, chunk * LANE * j:chunk * LANE * (j + 1)]
+            y = jnp.dot(both, x, preferred_element_type=jnp.float32)
+            y = y[:count] + y[count:]
+            for b in range(chunk):
+                spread_out[pl.ds(r0 * PITCH + j * chunk + b, count, stride=PITCH), :] = y[:, LANE * b:LANE * (b + 1)]
+        lines = pl.ds(r0 * blocks, count * blocks)
+        wide = spread_out[pl.ds(r0 * PITCH, count * PITCH), :].reshape(count, PITCH, LANE)[:, :blocks]
+        packed[lines, :] = wide.reshape(count * blocks, LANE).astype(jnp.bfloat16)
+        c = pltpu.make_async_copy(packed.at[lines], out_hbm.at[lines], out_sems.at[len(stores)])
+        c.start()
+        stores.append(c)
+
+    load.wait()
+    parts_of = [mean[h, k] for h in range(2) for k in range(mean.shape[1])]
+    e = (mean.shape[2] - 1) // 2
+    cross = jnp.concatenate([v[:e] for v in parts_of], axis=0)
+    mixed = jnp.concatenate([v[e:2 * e] for v in parts_of], axis=0)
+    line = sum(v[2 * e:] for v in parts_of[1:]) + parts_of[0][2 * e:]
+    er = lax.broadcasted_iota(jnp.int32, (top, top), 0)
+    ec = lax.broadcasted_iota(jnp.int32, (top, top), 1)
+    turned = mixed.T
+    work[:top, :top] = jnp.where(er >= ec, mixed, turned)
+    work[:top, top:n] = cross.T
+    work[top:, :top] = cross
+    work[top:, top:n] = jnp.where(er == ec, line, jnp.where(ec > er, mixed, turned))
     for p in range(steps):
         r0 = PANEL * p
         first = r0 // LANE
@@ -85,46 +136,47 @@
         if r1 < n:
             high, mid, low = parts(whole)
             right = jnp.concatenate([high, high, high, mid, mid, low], axis=0)
-            lh, lm, ll = parts(lower)
-            lhs = jnp.concatenate([lh, lm, ll, lh, lm, lh], axis=1)
+            lh, lm, ll = parts(upper)
+            lhs = jnp.concatenate([lh, lm, ll, lh, lm, lh], axis=0).T
             off = LANE * first
             for s0, s1 in ((r1, r1 + PANEL), (r1 + PANEL, n)):
                 if s0 < s1:
                     change = jnp.dot(lhs[s0 - off:s1 - off], right, preferred_element_type=jnp.float32)
                     at = LANE * tiles[0]
                     work[s0:s1, at:at + LANE * len(tiles)] -= change
-    inverse = work[:, n:]
-    high = inverse.astype(jnp.bfloat16)
-    mid = (inverse - high.astype(jnp.float32)).astype(jnp.bfloat16)
-    cells = feat_ref.shape[1]
-    blocks = cells // LANE
-    chunk = 4
-    for j in range(blocks // chunk):
-        x = feat_ref[:, chunk * LANE * j:chunk * LANE * (j + 1)]
-        y = jnp.dot(high, x, preferred_element_type=jnp.float32)
-        y = y + jnp.dot(mid, x, preferred_element_type=jnp.float32)
-        for b in range(chunk):
-            spread_out[pl.ds(j * chunk + b, n, stride=blocks), :] = y[:, LANE * b:LANE * (b + 1)]
-    out_ref[...] = spread_out[...].astype(jnp.bfloat16)
-
-
-def factor_and_solve(gram, features):
+        if p == top // PANEL - 1:
+            fetch.wait()
+        if p >= top // PANEL and p < steps - 1:
+            part = {4: (0, 32), 5: (32, 64), 6: (64, 128)}[p]
+            apply(part[0], part[1], top)
+    for r0 in range(top, n, n // 4):
+        apply(r0, r0 + n // 4, n)
+    for c in stores:
+        c.wait()
+
+
+def factor_and_solve(mean, features):
     n, cells = features.shape
     lines = n * cells // LANE
+    dma = pltpu.SemaphoreType.DMA
     return pl.pallas_call(
         factor_kernel,
         out_shape=(
             jax.ShapeDtypeStruct((n, n), jnp.float32),
             jax.ShapeDtypeStruct((lines, LANE), jnp.bfloat16),
         ),
-        in_specs=[pl.BlockSpec(memory_space=pltpu.VMEM)] * 2,
-        out_specs=(pl.BlockSpec(memory_space=pltpu.VMEM),) * 2,
+        in_specs=[pl.BlockSpec(memory_space=pl.ANY)] * 2,
+        out_specs=(pl.BlockSpec(memory_space=pltpu.VMEM), pl.BlockSpec(memory_space=pl.ANY)),
         scratch_shapes=[
+            pltpu.VMEM(mean.shape, jnp.float32),
             pltpu.VMEM((n, 2 * n), jnp.float32),
-            pltpu.VMEM((lines, LANE), jnp.float32),
+            pltpu.VMEM((n, cells), jnp.bfloat16),
+            pltpu.VMEM((n * PITCH, LANE), jnp.float32),
+            pltpu.VMEM((lines, LANE), jnp.bfloat16),
+            dma, dma, dma((8,)),
         ],
-        compiler_params=pltpu.CompilerParams(vmem_limit_bytes=48 << 20),
-    )(gram, features)
+        compiler_params=pltpu.CompilerParams(vmem_limit_bytes=62 << 20),
+    )(mean, features)
 
 
 def spread_mix(mix, snaps, fields, rows):
@@ -147,10 +199,10 @@
 
 
 def gram_kernel(
-    dims, side, steps, count, u_hbm, mix_ref, feat_hbm, out_ref,
-    u_ref, feat, weights, to_left, to_right, lo, hi,
+    dims, side, steps, count, u_hbm, mix_ref, feat_hbm, out_hbm,
+    u_ref, cells, feat, weights, lo, hi,
     stack, pair_in, mine, got_a, got_b, got_y, whole,
-    u_sem, feat_sem, l_send, l_recv, r_send, r_recv,
+    u_sem, feat_sem, out_sem, l_send, l_recv, r_send, r_recv,
     pair_send, pair_recv, a_send, a_recv, b_send, b_recv,
     y_send, y_recv, g_send, g_recv, f_send, f_recv,
 ):
@@ -168,8 +220,8 @@
     b = (1 - core) * z + core * x
     a_step = (1 - core) + core * side
     b_step = (1 - core) * side + core
-    half = stack.shape[1]
-    piece = half // side
+    far = sorted(range(1, side), key=lambda d: -min(d, side - d))
+    far_t = sorted(range(1, steps), key=lambda d: -min(d, steps - d))
 
     def at_a(k):
         return {"rows": 2 * (k * a_step + b * b_step) + core}
@@ -205,20 +257,12 @@
         weights[:, rows * i:rows * (i + 1)] = w
 
     def at(x, y):
-        return u_ref[pl.ds(x * ny + y, fs, stride=nx * ny), :]
+        j = x * ny + y
+        return cells[fs * j:fs * (j + 1), :]
 
     load.wait()
-    for y in range(ny):
-        to_left[fs * y:fs * (y + 1), :] = at(0, y)
-        to_right[fs * y:fs * (y + 1), :] = at(nx - 1, y)
-
-    pl.semaphore_wait(barrier, 2 * (side - 1) + steps + 2)
-
-    go_left = copy(to_left, hi, l_send, l_recv, left)
-    go_right = copy(to_right, lo, r_send, r_recv, right)
-    go_left.start()
-    go_right.start()
-    sends = [go_left, go_right]
+    for j in range(nx * ny):
+        cells[fs * j:fs * (j + 1), :] = u_ref[pl.ds(j, fs, stride=nx * ny), :]
 
     lane = lax.broadcasted_iota(jnp.int32, (fs, LANE), 1)
     zero = jnp.zeros((fs, LANE), jnp.float32)
@@ -249,7 +293,20 @@
         values = jnp.dot(weights[...], jnp.concatenate(columns, axis=1), preferred_element_type=jnp.float32)
         feat[:, ny * LANE * x:ny * LANE * (x + 1)] = values.astype(jnp.bfloat16)
 
-    for x in range(1, nx - 1):
+    ahead = 2
+    for x in range(1, 1 + ahead):
+        plane(x, lambda y: at(x - 1, y), lambda y: at(x + 1, y))
+
+    pl.semaphore_wait(barrier, 2 * (side - 1) + steps + 2)
+
+    block = fs * ny
+    go_left = copy(cells.at[pl.ds(0, block)], hi, l_send, l_recv, left)
+    go_right = copy(cells.at[pl.ds(block * (nx - 1), block)], lo, r_send, r_recv, right)
+    go_left.start()
+    go_right.start()
+    sends = [go_left, go_right]
+
+    for x in range(1 + ahead, nx - 1):
         plane(x, lambda y: at(x - 1, y), lambda y: at(x + 1, y))
 
     go_right.wait_recv()
@@ -267,39 +324,45 @@
 
     keep = pltpu.make_async_copy(feat, feat_hbm, feat_sem)
     keep.start()
-    edge = out_ref.shape[0] // 2
-    cut = edge // 2
     f = feat[...]
     gram = lax.dot_general(f, f, (((1,), (1,)), ((), ())), preferred_element_type=jnp.float32)
-    stack[0, :edge] = gram[:edge, :edge]
-    stack[0, edge:] = gram[edge:edge + cut, :edge]
-    stack[1, :cut] = gram[edge + cut:, :edge]
-    stack[1, cut:] = gram[edge:, edge:]
+    edge = gram.shape[0] // 2
+    e = (stack.shape[2] - 1) // 2
+    er = lax.broadcasted_iota(jnp.int32, (edge, edge), 0)
+    ec = lax.broadcasted_iota(jnp.int32, (edge, edge), 1)
+    second = gram[edge:, edge:]
+    mixed = jnp.where(er >= ec, gram[:edge, :edge], second)
+    line = jnp.sum(jnp.where(er == ec, second, 0.0), axis=0, keepdims=True)
+    owner = lax.broadcasted_iota(jnp.int32, (1, edge), 1) // e
+    for i in range(2 * side):
+        stack[i // side, i % side, :e] = gram[edge + e * i:edge + e * (i + 1), :edge]
+        stack[i // side, i % side, e:2 * e] = mixed[e * i:e * (i + 1)]
+        stack[i // side, i % side, 2 * e:] = jnp.where(owner == i, line, 0.0)
 
     pair = copy(stack.at[1 - core], pair_in, pair_send, pair_recv, partner)
     pair.start()
     sends.append(pair)
     pair.wait_recv()
-    mine[...] = (stack[core] + pair_in[...]).reshape(mine.shape)
-
-    for d in range(1, side):
+    mine[...] = stack[core] + pair_in[...]
+
+    for d in far:
         k = (a + d) % side
         c = copy(mine.at[k], got_a.at[a], a_send.at[d], a_recv.at[a], at_a(k))
         c.start()
         sends.append(c)
     total = mine[a]
-    for d in range(1, side):
+    for d in far[::-1]:
         k = (a + d) % side
         copy(mine.at[a], got_a.at[k], a_send.at[d], a_recv.at[k], at_a(k)).wait_recv()
         total = total + got_a[k]
     got_b[b] = total
 
-    for d in range(1, side):
+    for d in far:
         k = (b + d) % side
         c = copy(got_b.at[b], got_b.at[b], b_send.at[d], b_recv.at[b], at_b(k))
         c.start()
         sends.append(c)
-    for d in range(1, side):
+    for d in far[::-1]:
         k = (b + d) % side
         copy(got_b.at[b], got_b.at[k], b_send.at[d], b_recv.at[k], at_b(k)).wait_recv()
     total = got_b[0]
@@ -307,7 +370,7 @@
         total = total + got_b[k]
     got_y[t] = total
 
-    for d in range(1, steps):
+    for d in far_t:
         k = t + d
 
         @pl.when(k < steps)
@@ -330,7 +393,7 @@
     def forward(k):
         return copy(whole.at[core, k], whole.at[core, k], f_send.at[k], f_recv.at[k], partner)
 
-    for d in range(1, side):
+    for d in far:
         k = (a + d) % side
         c = copy(whole.at[core, a], whole.at[core, a], g_send.at[d], g_recv.at[a], at_a(k))
         c.start()
@@ -338,7 +401,7 @@
     c = forward(a)
     c.start()
     sends.append(c)
-    for d in range(1, side):
+    for d in far[::-1]:
         k = (a + d) % side
         copy(whole.at[core, a], whole.at[core, k], g_send.at[d], g_recv.at[k], at_a(k)).wait_recv()
         c = forward(k)
@@ -349,14 +412,8 @@
             whole.at[core, k], whole.at[1 - core, k], f_send.at[k], f_recv.at[k], partner
         ).wait_recv()
 
-    first = whole[0].reshape(half, edge)
-    second = whole[1].reshape(half, edge)
-    out_ref[:edge, :edge] = first[:edge]
-    out_ref[edge:edge + cut, :edge] = first[edge:]
-    out_ref[edge + cut:, :edge] = second[:cut]
-    out_ref[edge:, edge:] = second[cut:]
-    out_ref[:edge, edge:] = jnp.concatenate([first[edge:], second[:cut]], axis=0).T
-
+    give = pltpu.make_async_copy(whole, out_hbm, out_sem)
+    give.start()
     for c in sends:
         c.wait_send()
     for d in range(1, steps):
@@ -366,6 +423,7 @@
         def _():
             copy(got_y.at[t], got_y.at[t], y_send.at[d], y_recv.at[t], at_t(k)).wait_send()
     keep.wait()
+    give.wait()
 
 
 def features_and_mean(fields, mix):
@@ -376,32 +434,30 @@
     cells = nx * ny * nz
     rows = 7 * nf * ns + 8
     edge = width // 2
-    half = 3 * edge // 2
-    piece = half // side
+    piece = (side, 2 * (edge // (2 * side)) + 1, edge)
     plane = nf * ns * ny
     dma = pltpu.SemaphoreType.DMA
     f32, bf16 = jnp.float32, jnp.bfloat16
     return pl.pallas_call(
         functools.partial(gram_kernel, (nf, ns, nx, ny), side, steps, cells * lax.axis_size("rows")),
-        out_shape=(jax.ShapeDtypeStruct((width, cells), bf16), jax.ShapeDtypeStruct((width, width), f32)),
+        out_shape=(jax.ShapeDtypeStruct((width, cells), bf16), jax.ShapeDtypeStruct((2,) + piece, f32)),
         in_specs=[pl.BlockSpec(memory_space=pl.ANY), pl.BlockSpec(memory_space=pltpu.VMEM)],
-        out_specs=(pl.BlockSpec(memory_space=pl.ANY), pl.BlockSpec(memory_space=pltpu.VMEM)),
+        out_specs=(pl.BlockSpec(memory_space=pl.ANY),) * 2,
         scratch_shapes=[
+            pltpu.VMEM((nf * ns * nx * ny, nz), f32),
             pltpu.VMEM((nf * ns * nx * ny, nz), f32),
             pltpu.VMEM((width, cells), bf16),
             pltpu.VMEM((width, 6 * rows), bf16),
             pltpu.VMEM((plane, nz), f32),
             pltpu.VMEM((plane, nz), f32),
-            pltpu.VMEM((plane, nz), f32),
-            pltpu.VMEM((plane, nz), f32),
-            pltpu.VMEM((2, half, edge), f32),
-            pltpu.VMEM((half, edge), f32),
-            pltpu.VMEM((side, piece, edge), f32),
-            pltpu.VMEM((side, piece, edge), f32),
-            pltpu.VMEM((side, piece, edge), f32),
-            pltpu.VMEM((steps, piece, edge), f32),
-            pltpu.VMEM((2, side, piece, edge), f32),
-            dma, dma, dma, dma, dma, dma,
+            pltpu.VMEM((2,) + piece, f32),
+            pltpu.VMEM(piece, f32),
+            pltpu.VMEM(piece, f32),
+            pltpu.VMEM(piece, f32),
+            pltpu.VMEM(piece, f32),
+            pltpu.VMEM((steps,) + piece[1:], f32),
+            pltpu.VMEM((2,) + piece, f32),
+            dma, dma, dma, dma, dma, dma, dma,
             dma, dma,
             dma((side,)), dma((side,)),
             dma((side,)), dma((side,)),

time: 66.6 us -> 59.5 us (0.89)
  Pallas kernels: 63.2 us -> 57.9 us
  local copies, waits for them, and re-layouts: 2.53 us -> 0 us
    pallas_call x1, Pallas kernels: 50.1 us -> 47 us  [features_and_mean(): pl.pallas_call(functools.partial(gram_kernel, (nf, ns, nx, ny), side, ste...]
    unnamed x4 -> x0, local copies, waits for them, and re-layouts: 2.53 us -> none
    pallas_call x1, Pallas kernels: 13.1 us -> 10.9 us  [factor_and_solve(): pl.pallas_call(factor_kernel, out_shape=(jax.ShapeDtypeStruct((n, n), jnp...]
where the time goes in v4:
time: 59.5 us; the launch traced here: 58.7 us
  Pallas kernels  57.9 us (97%)
  between operations  0.8 us (1%)
    pallas_call x1, Pallas kernels, features_and_mean(): pl.pallas_call(functools.partial(gram_kernel, (nf, ns, nx, ny), side, ste...  47 us
    pallas_call x1, Pallas kernels, factor_and_solve(): pl.pallas_call(factor_kernel, out_shape=(jax.ShapeDtypeStruct((n, n), jnp...  10.9 us

profile of v4, /device:TPU:113, one launch (start us, length us, event | category | flops | bytes accessed | tf_op | source)
XLA Modules:
  0.0 58.7 jit_solution(4919451031251246452)
XLA Ops:
  0.6 47.0 %shard_map.41 = (bf16[256,4096]{1,0:T(8,128)(2,1)}, f32[2,8,17,128]{3,2,1,0:T(8,128)}) custom-call(f32[1280,128]{1,0:T(8,128)} %bitcast.3, f32[32,35]{1,0:T(8,128)} %mix_ref.1), custom_call_target="tpu_custom_call" | custom-call | tf_op jit(solution)/shard_map/pallas_call | solution.py:441
  47.7 10.9 %shard_map.42 = (f32[256,256]{1,0:T(8,128)}, bf16[8192,128]{1,0:T(8,128)(2,1)}) custom-call(f32[2,8,17,128]{3,2,1,0:T(8,128)} %get-tuple-element.6.mean_hbm, bf16[256,4096]{1,0:T(8,128)(2,1)} %get-tuple-element.7.feat_hbm), custom_call_target="tpu_custom_call" | custom-call | tf_op jit(solution)/shard_map/pallas_call | solution.py:162

commit v5 on v4

--- a/solution.py
+++ b/solution.py
@@ -32,7 +32,12 @@
         lane = (col0 + ROW * k) % LANE
         tc = tiles.index((col0 + ROW * k) // LANE)
         cols = [
-            [jnp.broadcast_to(rows[i][tc][:, lane + q:lane + q + 1], (ROW, LANE)) for i in range(k, count)]
+            [
+                jnp.take_along_axis(
+                    rows[i][tc], jnp.full((ROW, LANE), lane + q, jnp.int32), axis=1, mode="promise_in_bounds"
+                )
+                for i in range(k, count)
+            ]
             for q in range(ROW)
         ]
         scale = jnp.zeros((ROW, LANE), jnp.float32)

time: 59.5 us -> 57.8 us (0.971)
  Pallas kernels: 57.9 us -> 56.3 us
    pallas_call x1, Pallas kernels: 10.9 us -> 9.41 us  [factor_and_solve(): pl.pallas_call(factor_kernel, out_shape=(jax.ShapeDtypeStruct((n, n), jnp...]
where the time goes in v5:
time: 57.8 us; the launch traced here: 56.9 us
  Pallas kernels  56.3 us (97%)
  between operations  0.64 us (1%)
    pallas_call x1, Pallas kernels, features_and_mean(): pl.pallas_call(functools.partial(gram_kernel, (nf, ns, nx, ny), side, ste...  46.9 us
    pallas_call x1, Pallas kernels, factor_and_solve(): pl.pallas_call(factor_kernel, out_shape=(jax.ShapeDtypeStruct((n, n), jnp...  9.41 us

profile of v5, /device:TPU:113, one launch (start us, length us, event | category | flops | bytes accessed | tf_op | source)
XLA Modules:
  0.0 56.9 jit_solution(15455194530483640204)
XLA Ops:
  0.6 46.9 %shard_map.41 = (bf16[256,4096]{1,0:T(8,128)(2,1)}, f32[2,8,17,128]{3,2,1,0:T(8,128)}) custom-call(f32[1280,128]{1,0:T(8,128)} %bitcast.3, f32[32,35]{1,0:T(8,128)} %mix_ref.1), custom_call_target="tpu_custom_call" | custom-call | tf_op jit(solution)/shard_map/pallas_call | solution.py:446
  47.5 9.4 %shard_map.42 = (f32[256,256]{1,0:T(8,128)}, bf16[8192,128]{1,0:T(8,128)(2,1)}) custom-call(f32[2,8,17,128]{3,2,1,0:T(8,128)} %get-tuple-element.6.mean_hbm, bf16[256,4096]{1,0:T(8,128)(2,1)} %get-tuple-element.7.feat_hbm), custom_call_target="tpu_custom_call" | custom-call | tf_op jit(solution)/shard_map/pallas_call | solution.py:167

commit v6 on v5

--- a/solution.py
+++ b/solution.py
@@ -376,24 +376,17 @@
     got_y[t] = total
 
     for d in far_t:
-        k = t + d
-
-        @pl.when(k < steps)
-        def _():
-            copy(got_y.at[t], got_y.at[t], y_send.at[d], y_recv.at[t], at_t(k)).start()
-
-    whole[core, a] = jnp.zeros_like(total)
-    for k in range(steps):
-
-        @pl.when(k < t)
-        def _():
-            copy(got_y.at[k], got_y.at[k], y_send.at[0], y_recv.at[k], at_t(k)).wait_recv()
-
-        @pl.when(k <= t)
-        def _():
-            whole[core, a] += got_y[k]
-
-    whole[core, a] = whole[core, a] / ((t + 1).astype(jnp.float32) * jnp.float32(count))
+        k = (t + d) % steps
+        c = copy(got_y.at[t], got_y.at[t], y_send.at[d], y_recv.at[t], at_t(k))
+        c.start()
+        sends.append(c)
+    for d in far_t[::-1]:
+        k = (t + d) % steps
+        copy(got_y.at[t], got_y.at[k], y_send.at[d], y_recv.at[k], at_t(k)).wait_recv()
+    total = got_y[0]
+    for k in range(1, steps):
+        total = total + jnp.where(k <= t, got_y[k], 0.0)
+    whole[core, a] = total / ((t + 1).astype(jnp.float32) * jnp.float32(count))
 
     def forward(k):
         return copy(whole.at[core, k], whole.at[core, k], f_send.at[k], f_recv.at[k], partner)
@@ -421,12 +414,6 @@
     give.start()
     for c in sends:
         c.wait_send()
-    for d in range(1, steps):
-        k = t + d
-
-        @pl.when(k < steps)
-        def _():
-            copy(got_y.at[t], got_y.at[t], y_send.at[d], y_recv.at[t], at_t(k)).wait_send()
     keep.wait()
     give.wait()
 

time: 57.8 us -> 61.7 us (1.067)
  the two profiles are of different devices: /device:TPU:113 before, /device:TPU:1 now
where the time goes in v6:
time: 61.7 us; the launch traced here: 61.4 us
  Pallas kernels  60.8 us (99%)
  between operations  0.64 us (1%)
    pallas_call x1, Pallas kernels, features_and_mean(): pl.pallas_call(functools.partial(gram_kernel, (nf, ns, nx, ny), side, ste...  51.4 us
    pallas_call x1, Pallas kernels, factor_and_solve(): pl.pallas_call(factor_kernel, out_shape=(jax.ShapeDtypeStruct((n, n), jnp...  9.42 us

profile of v6, /device:TPU:1, one launch (start us, length us, event | category | flops | bytes accessed | tf_op | source)
XLA Modules:
  0.0 61.4 jit_solution(15831731928132641141)
XLA Ops:
  0.6 51.4 %shard_map.41 = (bf16[256,4096]{1,0:T(8,128)(2,1)}, f32[2,8,17,128]{3,2,1,0:T(8,128)}) custom-call(f32[1280,128]{1,0:T(8,128)} %bitcast.3, f32[32,35]{1,0:T(8,128)} %mix_ref.1), custom_call_target="tpu_custom_call" | custom-call | tf_op jit(solution)/shard_map/pallas_call | solution.py:433
  52.0 9.4 %shard_map.42 = (f32[256,256]{1,0:T(8,128)}, bf16[8192,128]{1,0:T(8,128)(2,1)}) custom-call(f32[2,8,17,128]{3,2,1,0:T(8,128)} %get-tuple-element.6.mean_hbm, bf16[256,4096]{1,0:T(8,128)(2,1)} %get-tuple-element.7.feat_hbm), custom_call_target="tpu_custom_call" | custom-call | tf_op jit(solution)/shard_map/pallas_call | solution.py:167
